TPU v7x, 128 devices: a whole 4x4x4 slice. The times are simulated.
128 devices in a mesh: row: 4 (over z), col: 8 (over x_hi, y), tp: 4 (over x_lo, core).
Axes of the slice: x: 4 (x_hi: 2, x_lo: 2; x = x_hi * 2 + x_lo), y: 4, z: 4, core: 2. Of those that a mesh axis runs over, the one named last changes fastest.
Arguments:
- tokens: bfloat16 [32, 128, 3200], P('row', 'col', 'tp'), may hold values from -6 to 6
- cotangent: bfloat16 [32, 128, 3200], P('row', 'col', 'tp'), may hold values from -6 to 6
- expand_weight: bfloat16 [3200, 6400], P(None, 'tp'), may hold values from -0.10606602 to 0.10606602
- reduce_weight: bfloat16 [3200, 6400], P(None, 'tp'), may hold values from -0.075 to 0.075
- position_kernel: float32 [3, 3, 3200], replicated, may hold values from -1.5 to 1.5
- norm_gain: float32 [3200], replicated, may hold values from 0.2 to 2.4
Outputs:
- grad_tokens: bfloat16 [32, 128, 3200], P('row', 'col', 'tp')
- grad_expand: float32 [3200, 6400], P(('row', 'col'), 'tp')
- grad_reduce: float32 [3200, 6400], P(('row', 'col'), 'tp')
- grad_kernel: float32 [3, 3, 3200], P(None, None, 'tp')
- grad_gain: float32 [3200], P('tp')
All inputs are finite; a program needn't handle non-finite values.
Results may differ from a plain program's by a relative error of at most 0.029.
Values may be sent and summed in bfloat16 or wider, within the bound.
A program may use at most 192 MiB of HBM per device.

v0:
```python
import jax
import jax.numpy as jnp
from jax import lax
from jax.sharding import PartitionSpec as P

epsilon = 1e-06


def padded_2(cells, sides, width):
    for axis, dim in sides:
        count = lax.axis_size(axis)
        ends = count - 1
        head = lax.slice_in_dim(cells, 0, width, axis=dim)
        tail = lax.slice_in_dim(cells, cells.shape[dim] - width, cells.shape[dim], axis=dim)
        cells = jnp.concatenate(
            [
                lax.ppermute(tail, axis, [(i, (i + 1) % count) for i in range(ends)]),
                cells,
                lax.ppermute(head, axis, [((i + 1) % count, i) for i in range(ends)]),
            ],
            axis=dim,
        )
    return cells


def conv_forward(padded, kernel, row_cells, col_cells):
    summed = jnp.zeros((row_cells, col_cells, padded.shape[2]), jnp.float32)
    for row_shift in range(3):
        for col_shift in range(3):
            summed = (
                summed
                + kernel[row_shift, col_shift]
                * padded[row_shift : row_shift + row_cells, col_shift : col_shift + col_cells]
            )
    return summed


def conv_back(padded, kernel, row_cells, col_cells):
    summed = jnp.zeros((row_cells, col_cells, padded.shape[2]), jnp.float32)
    for row_shift in range(3):
        for col_shift in range(3):
            summed = (
                summed
                + kernel[row_shift, col_shift]
                * padded[
                    2 - row_shift : 2 - row_shift + row_cells,
                    2 - col_shift : 2 - col_shift + col_cells,
                ]
            )
    return summed


def kernel_terms(grad_field, padded, row_cells, col_cells):
    pieces = []
    for row_shift in range(3):
        for col_shift in range(3):
            pieces.append(
                jnp.sum(
                    grad_field
                    * padded[row_shift : row_shift + row_cells, col_shift : col_shift + col_cells],
                    axis=(0, 1),
                )
            )
    return jnp.stack(pieces).reshape(3, 3, grad_field.shape[2])


def gelu_slope(pre_act):
    cdf = 0.5 * (1.0 + lax.erf(pre_act * 0.7071067811865476))
    density = jnp.exp(-0.5 * pre_act * pre_act) * 0.3989422804014327
    return cdf + pre_act * density


def on_device(tokens, cotangent, expand_weight, reduce_weight, position_kernel, norm_gain):
    row_cells, col_cells, quarter = tokens.shape
    feature_width = quarter * lax.axis_size("tp")
    offset = lax.axis_index("tp") * quarter
    grid_devices = lax.axis_size("row") * lax.axis_size("col")
    factor = float(row_cells * col_cells * grid_devices) ** (-0.5)
    own_kernel = lax.dynamic_slice_in_dim(position_kernel, offset, quarter, 2)
    own_gain = lax.dynamic_slice_in_dim(norm_gain, offset, quarter, 0)
    padded_x = padded_2(tokens, (("row", 0), ("col", 1)), 1)
    own_h = (
        tokens.astype(jnp.float32)
        + conv_forward(padded_x.astype(jnp.float32), own_kernel, row_cells, col_cells)
    ).astype(jnp.bfloat16)
    whole_h, full_cot = (
        lax.all_gather(own_h, "tp", axis=2, tiled=True),
        lax.all_gather(cotangent, "tp", axis=2, tiled=True),
    )
    flat_cot = full_cot.reshape(row_cells * col_cells, feature_width)
    d_act = jnp.dot(flat_cot, reduce_weight, preferred_element_type=jnp.float32)
    h_float = whole_h.astype(jnp.float32)
    inverse = lax.rsqrt(jnp.mean(h_float * h_float, axis=-1, keepdims=True) + epsilon)
    normed = (
        (h_float * inverse * norm_gain)
        .astype(jnp.bfloat16)
        .reshape(row_cells * col_cells, feature_width)
    )
    pre_act = jnp.dot(normed, expand_weight, preferred_element_type=jnp.float32)
    activated = jax.nn.gelu(pre_act, approximate=False).astype(jnp.bfloat16)
    d_pre = (d_act * gelu_slope(pre_act)).astype(jnp.bfloat16)
    hidden_part = expand_weight.shape[1]
    d_norm = lax.dot_general(
        d_pre, expand_weight, (((1,), (1,)), ((), ())), preferred_element_type=jnp.float32
    )
    d_norm = d_norm.reshape(row_cells, col_cells, feature_width)
    own_hf = own_h.astype(jnp.float32)
    own_dn = lax.psum_scatter(
        d_norm.astype(jnp.bfloat16), "tp", scatter_dimension=2, tiled=True
    ).astype(jnp.float32)
    inner_dot = lax.psum(jnp.sum(own_dn * own_gain * own_hf, axis=-1, keepdims=True), "tp")
    scaled = own_dn * own_gain
    d_mlp = inverse * scaled - own_hf * inverse**3 * inner_dot / feature_width
    d_hidden = (cotangent.astype(jnp.float32) + d_mlp).astype(jnp.bfloat16)
    padded_dh = padded_2(d_hidden, (("row", 0), ("col", 1)), 1)
    dh_float = d_hidden.astype(jnp.float32)
    grad_tokens = (
        dh_float + conv_back(padded_dh.astype(jnp.float32), own_kernel, row_cells, col_cells)
    ).astype(jnp.bfloat16)
    both_grads = lax.psum_scatter(
        jnp.concatenate(
            [
                lax.dot_general(
                    normed, d_pre, (((0,), (0,)), ((), ())), preferred_element_type=jnp.float32
                )
                * factor,
                lax.dot_general(
                    flat_cot,
                    activated,
                    (((0,), (0,)), ((), ())),
                    preferred_element_type=jnp.float32,
                )
                * factor,
            ],
            axis=1,
        ).astype(jnp.bfloat16),
        ("row", "col"),
        scatter_dimension=0,
        tiled=True,
    ).astype(jnp.float32)
    grad_expand = both_grads[:, :hidden_part]
    grad_reduce = both_grads[:, hidden_part:]
    local_gain = jnp.sum(own_dn * own_hf * inverse, axis=(0, 1)) * factor
    local_kernel = (
        kernel_terms(dh_float, padded_x.astype(jnp.float32), row_cells, col_cells) * factor
    )
    grad_gain, grad_kernel = lax.psum((local_gain, local_kernel), ("row", "col"))
    return (grad_tokens, grad_expand, grad_reduce, grad_kernel, grad_gain)


def solution(mesh):
    placed = (P("row", "col", "tp"), P("row", "col", "tp"), P(None, "tp"), P(None, "tp"), P(), P())
    return jax.shard_map(
        on_device,
        mesh=mesh,
        in_specs=placed,
        out_specs=(
            P("row", "col", "tp"),
            P(("row", "col"), "tp"),
            P(("row", "col"), "tp"),
            P(None, None, "tp"),
            P("tp"),
        ),
        check_vma=False,
    )
```

profile of v0, /device:TPU:0, one launch (start us, length us, event | category | flops | bytes accessed | tf_op | source)
XLA Modules:
  0.0 673.6 jit_solution(9972905049139235258)
XLA Ops:
  8.9 3.9 collective-permute-start
  12.8 1.3 collective-permute-start.1
  14.1 2.9 copy.81
  18.6 1.3 collective-permute-start.3
  19.9 4.5 collective-permute-start.2
  24.5 40.4 %all_gather.7 = bf16[8,16,3200]{1,0,2:T(8,128)(2,1)} all-gather(bf16[8,16,800]{1,0,2:T(8,128)(2,1)S(1)} %copy.81), channel_id=1, replica_groups=mesh['row'=4,'col'=8,'tp'=4] {'tp'}, dimensions={2}, use_global_device_ids=true | all-gather | bytes 1024000 | tf_op jit(solution)/shard_map/all_gather | solution.py:88
  64.9 6.1 copy.82
  73.1 2.0 copy.79
  75.1 40.8 %all_gather.6 = bf16[8,16,3200]{1,0,2:T(8,128)(2,1)} all-gather(bf16[8,16,800]{1,0,2:T(8,128)(2,1)S(1)} %copy.79), channel_id=1, replica_groups=mesh['row'=4,'col'=8,'tp'=4] {'tp'}, dimensions={2}, use_global_device_ids=true | all-gather | bytes 1024000 | tf_op jit(solution)/shard_map/all_gather | solution.py:87
  115.9 6.1 copy.80
  123.8 5.6 fusion.112
  130.4 7.0 %fusion = bf16[3200,1600]{0,1:T(8,128)(2,1)} fusion(bf16[128,3200]{1,0:T(8,128)(2,1)S(1)} %bitcast.27, f32[128,1600]{0,1:T(8,128)S(1)} %fusion.112), kind=kOutput, calls=%fused_computation.3 | convolution fusion | flops 1334272000 | bytes 11878400 | tf_op jit(solution)/shard_map/dot_general | solution.py:127
  137.4 4.2 fusion.1
  141.6 1.7 convolution_convert_fusion
  143.4 5.3 multiply_convert_fusion.1
  148.7 5.6 copy.89
  154.3 8.2 %reshape.40 = bf16[3200,128]{1,0:T(8,128)(2,1)} reshape(bf16[3200,8,16]{2,1,0:T(8,128)(2,1)} %bitcast.21) | data formatting | bytes 1638400
  162.8 21.7 %pad_maximum_fusion = bf16[3200,3200]{0,1:T(8,128)(2,1)} fusion(bf16[3200,1600]{0,1:T(8,128)(2,1)} %fusion, bf16[3200,1600]{0,1:T(8,128)(2,1)} %multiply_convert_fusion.1), kind=kLoop, calls=%fused_computation | loop fusion | flops 40960000 | bytes 40960000 | tf_op jit(solution)/shard_map/concatenate | solution.py:121
  186.7 2.1 reshape.41
  188.9 1.9 copy.90
  190.9 6.2 psum.21
  197.8 1.3 collective-permute-start.5
  199.1 4.6 collective-permute-start.4
  203.9 213.0 %collective-permute-done.4 = bf16[1,16,800]{2,1,0:T(8,128)(2,1)S(1)} collective-permute-done((bf16[1,16,800]{2,1,0:T(8,128)(2,1)S(1)}, bf16[1,16,800]{2,1,0:T(8,128)(2,1)S(1)}, u32[]{:S(2)}, u32[]{:S(2)}) %collective-permute-start.4) | collective-permute-done | bytes 25632 | tf_op jit(solution)/shard_map/ppermute | solution.py:17
  417.0 1.3 collective-permute-start.7
  418.3 4.5 collective-permute-start.6
  422.8 177.0 %all-reduce.1 = (f32[3,3,800]{2,1,0:T(4,128)}, f32[800]{0:T(1024)}) all-reduce(f32[3,3,800]{2,1,0:T(4,128)S(1)} %mul.381, f32[800]{0:T(1024)S(1)} %broadcast_multiply_fusion.1), channel_id=1, replica_groups=mesh['row'=4,'col'=8,'tp'=4] {'row','col'}, use_global_device_ids=true, to_apply=%region_14.0 | all-reduce | flops 8000 | bytes 64000 | tf_op jit(solution)/shard_map/psum | solution.py:147
  600.2 1.1 fusion.28
  601.2 60.7 %all-reduce.4.cloned.1.call-done = bf16[3200,3200]{0,1:T(8,128)(2,1)} async-done(((bf16[3200,3200]{0,1:T(8,128)(2,1)}), bf16[3200,3200]{0,1:T(8,128)(2,1)}) %all-reduce.4.cloned.1.call-update) | async-done | bytes 20480016
  661.9 1.7 dynamic-slice_convert_fusion
  663.8 1.2 copy.87
  664.9 1.2 copy.88
  (108 shorter events, 10.5 us)
Async XLA Ops:
  8.0 64.7 %copy-start.1 = (bf16[8,16,800]{2,1,0:T(8,128)(2,1)S(1)}, bf16[8,16,800]{2,1,0:T(8,128)(2,1)}, u32[]{:S(2)}) copy-start(bf16[8,16,800]{2,1,0:T(8,128)(2,1)} %param.6) | copy-start | bytes 614404
  8.0 178.7 %reduce-scatter.5.cloned.1.call-start = ((), (), s32[]{:S(2)}) async-start(), calls=%async_computation.1 | async-start | bytes 1024000
  8.9 8.1 %collective-permute-start = (bf16[1,16,800]{2,1,0:T(8,128)(2,1)S(1)}, bf16[1,16,800]{2,1,0:T(8,128)(2,1)S(1)}, u32[]{:S(2)}, u32[]{:S(2)}) collective-permute-start(bf16[1,16,800]{2,1,0:T(8,128)(2,1)S(1)} %get-tuple-element.67), channel_id=1, source_target_pairs={{0,32},{32,64},{64,96},{1,33},{33,65},{65,97},{2,34},{34,66},{66,9... | collective-permute-start | bytes 76808 | tf_op jit(solution)/shard_map/ppermute | solution.py:17
  12.8 5.8 collective-permute-start.1
  18.6 53.5 %collective-permute-start.3 = (bf16[10,1,800]{2,0,1:T(8,128)(2,1)S(1)}, bf16[10,1,800]{2,0,1:T(8,128)(2,1)S(1)}, u32[]{:S(2)}, u32[]{:S(2)}) collective-permute-start(bf16[10,1,800]{2,0,1:T(8,128)(2,1)S(1)} %copy.94), channel_id=1, source_target_pairs={{4,0},{8,4},{12,8},{16,12},{20,16},{24,20},{28,24},{5,1},{9,5},{13... | collective-permute-start | bytes 48008 | tf_op jit(solution)/shard_map/ppermute | solution.py:19
  19.9 52.2 %collective-permute-start.2 = (bf16[10,1,800]{2,0,1:T(8,128)(2,1)S(1)}, bf16[10,1,800]{2,0,1:T(8,128)(2,1)S(1)}, u32[]{:S(2)}, u32[]{:S(2)}) collective-permute-start(bf16[10,1,800]{2,0,1:T(8,128)(2,1)S(1)} %copy.93), channel_id=1, source_target_pairs={{0,4},{4,8},{8,12},{12,16},{16,20},{20,24},{24,28},{1,5},{5,9},{9,... | collective-permute-start | bytes 48008 | tf_op jit(solution)/shard_map/ppermute | solution.py:17
  72.1 0.6 copy-start.13
  72.1 0.6 copy-start.17
  72.1 49.9 %copy-start.3 = (f32[800]{0:T(1024)}, f32[800]{0:T(1024)S(1)}, u32[]{:S(2)}) copy-start(f32[800]{0:T(1024)S(1)} %get-tuple-element.47) | copy-start | bytes 9604
  123.8 13.6 %slice-start.3 = ((s8[10240000]{0:T(1024)(128)(4,1)}), s8[4194304]{0:T(1024)(128)(4,1)S(1)}, s32[]{:S(2)}) async-start(s8[10240000]{0:T(1024)(128)(4,1)} %bitcast.22), calls=%async_computation.6 | async-start | bytes 8388608
  123.8 17.8 %slice-start = ((s8[10240000]{0:T(1024)(128)(4,1)}), s8[4194304]{0:T(1024)(128)(4,1)S(1)}, s32[]{:S(2)}) async-start(s8[10240000]{0:T(1024)(128)(4,1)} %bitcast.19), calls=%async_computation.3 | async-start | bytes 8388608
  129.5 0.9 copy-start
  130.4 7.0 %slice-start.4 = ((s8[10240000]{0:T(1024)(128)(4,1)}), s8[4194304]{0:T(1024)(128)(4,1)S(1)}, s32[]{:S(2)}) async-start(s8[10240000]{0:T(1024)(128)(4,1)} %bitcast.22), calls=%async_computation.7 | async-start | bytes 8388608
  130.4 7.0 %slice-start.5 = ((s8[10240000]{0:T(1024)(128)(4,1)}), s8[1851392]{0:T(1024)(128)(4,1)S(1)}, s32[]{:S(2)}) async-start(s8[10240000]{0:T(1024)(128)(4,1)} %bitcast.22), calls=%async_computation.8 | async-start | bytes 3702784
  130.4 11.2 %slice-start.1 = ((s8[10240000]{0:T(1024)(128)(4,1)}), s8[4194304]{0:T(1024)(128)(4,1)S(1)}, s32[]{:S(2)}) async-start(s8[10240000]{0:T(1024)(128)(4,1)} %bitcast.19), calls=%async_computation.4 | async-start | bytes 8388608
  130.4 11.2 %slice-start.2 = ((s8[10240000]{0:T(1024)(128)(4,1)}), s8[1851392]{0:T(1024)(128)(4,1)S(1)}, s32[]{:S(2)}) async-start(s8[10240000]{0:T(1024)(128)(4,1)} %bitcast.19), calls=%async_computation.5 | async-start | bytes 3702784
  162.5 499.4 %all-reduce.4.cloned.1.call-start = ((), (), s32[]{:S(2)}) async-start(), calls=%async_computation.2 | async-start | bytes 40960000
  184.5 1.0 copy-start.20
  184.5 12.6 %copy-start.2 = (bf16[8,16,800]{2,1,0:T(8,128)(2,1)S(1)}, bf16[8,16,800]{2,1,0:T(8,128)(2,1)}, u32[]{:S(2)}) copy-start(bf16[8,16,800]{2,1,0:T(8,128)(2,1)} %param.7) | copy-start | bytes 614404
  184.5 12.6 %copy-start.19 = (f32[8,16]{1,0:T(8,128)S(1)}, f32[8,16]{1,0:T(8,128)}, u32[]{:S(2)}) copy-start(f32[8,16]{1,0:T(8,128)} %get-tuple-element.68) | copy-start | bytes 1540
  184.5 415.6 %copy-start.4 = (f32[800]{0:T(1024)S(1)}, f32[800]{0:T(1024)}, u32[]{:S(2)}) copy-start(f32[800]{0:T(1024)} %copy-done.3) | copy-start | bytes 9604
  184.5 415.6 %copy-start.6 = (f32[800]{0:T(1024)S(1)}, f32[800]{0:T(1024)}, u32[]{:S(2)}) copy-start(f32[800]{0:T(1024)} %copy-done.5) | copy-start | bytes 9604
  184.6 415.6 %copy-start.8 = (f32[800]{0:T(1024)S(1)}, f32[800]{0:T(1024)}, u32[]{:S(2)}) copy-start(f32[800]{0:T(1024)} %copy-done.7) | copy-start | bytes 9604
  184.6 415.6 %copy-start.10 = (f32[800]{0:T(1024)S(1)}, f32[800]{0:T(1024)}, u32[]{:S(2)}) copy-start(f32[800]{0:T(1024)} %copy-done.9) | copy-start | bytes 9604
  184.6 415.6 %copy-start.12 = (f32[800]{0:T(1024)S(1)}, f32[800]{0:T(1024)}, u32[]{:S(2)}) copy-start(f32[800]{0:T(1024)} %copy-done.11) | copy-start | bytes 9604
  184.6 415.6 %copy-start.14 = (f32[800]{0:T(1024)S(1)}, f32[800]{0:T(1024)}, u32[]{:S(2)}) copy-start(f32[800]{0:T(1024)} %copy-done.13) | copy-start | bytes 9604
  184.6 415.6 %copy-start.16 = (f32[800]{0:T(1024)S(1)}, f32[800]{0:T(1024)}, u32[]{:S(2)}) copy-start(f32[800]{0:T(1024)} %copy-done.15) | copy-start | bytes 9604
  184.6 415.6 %copy-start.18 = (f32[800]{0:T(1024)S(1)}, f32[800]{0:T(1024)}, u32[]{:S(2)}) copy-start(f32[800]{0:T(1024)} %copy-done.17) | copy-start | bytes 9604
  197.8 6.1 collective-permute-start.5
  199.1 217.8 %collective-permute-start.4 = (bf16[1,16,800]{2,1,0:T(8,128)(2,1)S(1)}, bf16[1,16,800]{2,1,0:T(8,128)(2,1)S(1)}, u32[]{:S(2)}, u32[]{:S(2)}) collective-permute-start(bf16[1,16,800]{2,1,0:T(8,128)(2,1)S(1)} %get-tuple-element.64), channel_id=1, source_target_pairs={{0,32},{32,64},{64,96},{1,33},{33,65},{65,97},{2,34},{34,66},{66,9... | collective-permute-start | bytes 76808 | tf_op jit(solution)/shard_map/ppermute | solution.py:17
  417.0 182.9 %collective-permute-start.7 = (bf16[10,1,800]{2,0,1:T(8,128)(2,1)S(1)}, bf16[10,1,800]{2,0,1:T(8,128)(2,1)S(1)}, u32[]{:S(2)}, u32[]{:S(2)}) collective-permute-start(bf16[10,1,800]{2,0,1:T(8,128)(2,1)S(1)} %copy.84), channel_id=1, source_target_pairs={{4,0},{8,4},{12,8},{16,12},{20,16},{24,20},{28,24},{5,1},{9,5},{13... | collective-permute-start | bytes 48008 | tf_op jit(solution)/shard_map/ppermute | solution.py:19
  418.3 181.6 %collective-permute-start.6 = (bf16[10,1,800]{2,0,1:T(8,128)(2,1)S(1)}, bf16[10,1,800]{2,0,1:T(8,128)(2,1)S(1)}, u32[]{:S(2)}, u32[]{:S(2)}) collective-permute-start(bf16[10,1,800]{2,0,1:T(8,128)(2,1)S(1)} %copy.83), channel_id=1, source_target_pairs={{0,4},{4,8},{8,12},{12,16},{16,20},{20,24},{24,28},{1,5},{5,9},{9,... | collective-permute-start | bytes 48008 | tf_op jit(solution)/shard_map/ppermute | solution.py:17
  (5 other events, 3.0 us)
Sparse Core Ops, SparseCore 0:
  162.6 22.7 reduce-scatter.4
Sparse Core Ops, SparseCore 1:
  184.6 477.3 all-reduce.3
where the time goes:
time: 675 us; the launch traced here: 674 us
  waiting for transfers between devices  274 us (41%)
  blocking collectives  264 us (39%)
  local copies, waits for them, and re-layouts  43.2 us (6%)
  other arithmetic  28 us (4%)
  matrix products  23.8 us (4%)
  starting transfers between devices  23 us (3%)
  between operations  16.8 us (2%)
    ppermute x4, waiting for transfers between devices, padded_2(): lax.ppermute(tail, axis, [(i, (i + 1) % count) for i in range(ends)])  213 us
    psum x1, blocking collectives, on_device(): lax.psum((local_gain, local_kernel), ('row', 'col'))  177 us
    unnamed x4, waiting for transfers between devices  60.8 us
    all_gather x1, blocking collectives, on_device(): lax.all_gather(own_h, 'tp', axis=2, tiled=True)  40.8 us
    all_gather x1, blocking collectives, on_device(): lax.all_gather(cotangent, 'tp', axis=2, tiled=True)  40.4 us
    unnamed x66, local copies, waits for them, and re-layouts  25.9 us
    concatenate x1, other arithmetic, on_device(): jnp.concatenate([lax.dot_general(normed, d_pre, (((0,), (0,)), ((), ())),...  21.7 us
    ppermute x4, starting transfers between devices, padded_2(): lax.ppermute(tail, axis, [(i, (i + 1) % count) for i in range(ends)])  17.6 us
  transfers between devices with their start and end apart: 10, of which 3 were waited for; matrix products, arithmetic and copies ran while one was open for 6% of the time, Pallas kernels for 0%

commit v1 on v0

v1 whole, which is shorter than its diff:
```python
import jax
import jax.numpy as jnp
from jax import lax
from jax.experimental import pallas as pl
from jax.experimental.pallas import tpu as pltpu
from jax.sharding import PartitionSpec as P

MESH = pl.DeviceIdType.MESH
F32 = jnp.float32
BF16 = jnp.bfloat16
epsilon = 1e-06
ROWS, COLS, TOK = 8, 16, 128
DQ, D = 800, 3200
HD, HP, HQ = 1600, 1664, 400
NT = (((1,), (1,)), ((), ()))


def mul(value, by):
    return pl.multiple_of(value, by)


def kernel(
    tok_ref, cot_ref, w1_hbm, w2_hbm, pk_ref, gain_ref,
    gt_ref, ge_ref, gr_ref, kg_ref,
    w1, w2, padded, padded2, cot, pos, trans, pre, dact, inv, bt, b1, at, btile,
    e_send, e_recv, inn, erow, ecol, rrow, rcol, rcor, xs, xr, keep, ys, yr, kall,
    send_sem, recv_sem, local_sem, wsem,
):
    z = lax.axis_index("row")
    col = lax.axis_index("col")
    tp = lax.axis_index("tp")
    xh, y = col // 4, col % 4
    xl, core = tp // 2, tp % 2

    def at_y(d):
        return (z, xh * 4 + (y + d) % 4, tp)

    def at_z(d):
        return ((z + d) % 4, col, tp)

    def at_grid(dr, dc):
        return ((z + dr + 4) % 4, (col + dc + 8) % 8, tp)

    x_peer = (z, (1 - xh) * 4 + y, tp)
    tp_sib = xl * 2 + 1 - core
    tp_cross = (1 - xl) * 2 + core
    tp_far = (1 - xl) * 2 + 1 - core
    sib, cross, far = (z, col, tp_sib), (z, col, tp_cross), (z, col, tp_far)

    grid_steps = [(1, 0), (-1, 0), (0, 1), (0, -1), (1, 1), (1, -1), (-1, 1), (-1, -1)]
    peers = [at_grid(*s) for s in grid_steps]
    peers += [at_y(d) for d in (1, 2, 3)] + [at_z(d) for d in (1, 2, 3)]
    peers += [x_peer, sib, cross, far]
    barrier = pltpu.get_barrier_semaphore()
    for peer in peers:
        pl.semaphore_signal(barrier, inc=1, device_id=peer, device_id_type=MESH)

    counts = {"remote": 0, "local": 0}
    started = []

    def send(src, dst, to):
        k = counts["remote"]
        counts["remote"] += 1
        copy = pltpu.make_async_remote_copy(
            src_ref=src, dst_ref=dst, send_sem=send_sem.at[k], recv_sem=recv_sem.at[k],
            device_id=to, device_id_type=MESH,
        )
        copy.start()
        started.append(copy)
        return copy

    def local(src, dst):
        k = counts["local"]
        counts["local"] += 1
        copy = pltpu.make_async_copy(src, dst, local_sem.at[k])
        copy.start()
        return copy

    def arrived(copies):
        for copy in copies:
            copy.wait_recv()

    order = [tp, tp_sib, tp_cross, tp_far]
    w_copies = []
    for n, (src, dst) in enumerate(((w2_hbm, w2), (w1_hbm, w1))):
        for k, j in enumerate(order):
            rows = pl.ds(mul(j * DQ, 16), DQ)
            copy = pltpu.make_async_copy(src.at[rows], dst.at[rows], wsem.at[n * 4 + k])
            copy.start()
            w_copies.append(copy)

    def fill_edges(field, n):
        erow[n, 0] = field[1, 8:24, :]
        erow[n, 1] = field[8, 8:24, :]
        for i in range(ROWS):
            ecol[n, 0, i : i + 1, :] = field[i + 1, 8:9, :]
            ecol[n, 1, i : i + 1, :] = field[i + 1, 23:24, :]

    def send_edges(n):
        low, high = pl.ds(0, 8), pl.ds(8, 8)
        return [
            send(erow.at[n, 1], rrow.at[n, 0], at_grid(1, 0)),
            send(erow.at[n, 0], rrow.at[n, 1], at_grid(-1, 0)),
            send(ecol.at[n, 1], rcol.at[n, 0], at_grid(0, 1)),
            send(ecol.at[n, 0], rcol.at[n, 1], at_grid(0, -1)),
            send(erow.at[n, 1, high], rcor.at[n, 0], at_grid(1, 1)),
            send(erow.at[n, 1, low], rcor.at[n, 1], at_grid(1, -1)),
            send(erow.at[n, 0, high], rcor.at[n, 2], at_grid(-1, 1)),
            send(erow.at[n, 0, low], rcor.at[n, 3], at_grid(-1, -1)),
        ]

    one, zero = jnp.float32(1), jnp.float32(0)
    top = jnp.where(z > 0, one, zero)
    bottom = jnp.where(z < 3, one, zero)
    left = jnp.where(col > 0, one, zero)
    right = jnp.where(col < 7, one, zero)

    def fill_halo(field, n):
        field[0, 8:24, :] = rrow[n, 0] * top
        field[9, 8:24, :] = rrow[n, 1] * bottom
        for i in range(ROWS):
            field[i + 1, 7:8, :] = rcol[n, 0, i : i + 1, :] * left
            field[i + 1, 24:25, :] = rcol[n, 1, i : i + 1, :] * right
        field[0, 7:8, :] = rcor[n, 0, 7:8, :] * (top * left)
        field[0, 24:25, :] = rcor[n, 1, 0:1, :] * (top * right)
        field[9, 7:8, :] = rcor[n, 2, 7:8, :] * (bottom * left)
        field[9, 24:25, :] = rcor[n, 3, 0:1, :] * (bottom * right)

    for i in range(ROWS):
        padded[i + 1, 8:24, :] = tok_ref[i].astype(F32)
        cot[tp, i * COLS : (i + 1) * COLS, 0:DQ] = cot_ref[i]
    fill_edges(padded, 0)
    pl.semaphore_wait(barrier, len(peers))
    halo = send_edges(0)
    cot_sib = send(cot.at[tp], cot.at[tp], sib)
    cot_cross = send(cot.at[tp], cot.at[tp], cross)
    pre[:, 1536:1664] = jnp.zeros((TOK, 128), F32)
    dact[:, 1536:1664] = jnp.zeros((TOK, 128), F32)

    arrived(halo)
    fill_halo(padded, 0)

    def conv_row(i, carry):
        total = padded[i + 1, 8:24, :]
        for p in range(3):
            for q in range(3):
                total = total + pk_ref[tp, p * 3 + q : p * 3 + q + 1, :] * padded[i + p, 7 + q : 23 + q, :]
        pos[tp, pl.ds(mul(i * COLS, 16), COLS), 0:DQ] = total.astype(BF16)
        return carry

    lax.fori_loop(0, ROWS, conv_row, 0)
    pos_cross = send(pos.at[tp], pos.at[tp], cross)
    pos_sib = send(pos.at[tp], pos.at[tp], sib)

    def transpose_chunk(g, j, scale):
        source = pos if g else cot

        def tile(k, carry):
            lanes = pl.ds(mul(k * 128, 128), 128)
            part = source[j, :, lanes].astype(F32)
            if scale:
                part = part * gain_ref[j, 0:1, lanes]
            trans[g, j, lanes, :] = part.T.astype(BF16)
            return carry

        lax.fori_loop(0, 7, tile, 0)

    def act_chunk(k):
        j = order[k]
        w_copies[k].wait()
        part = jnp.dot(cot[j, :, 0:DQ], w2[pl.ds(mul(j * DQ, 16), DQ), :], preferred_element_type=F32)
        dact[:, 0:HD] = part if k == 0 else dact[:, 0:HD] + part
        transpose_chunk(0, j, False)

    def pre_chunk(k):
        j = order[k]
        w_copies[4 + k].wait()
        value = pos[j, :, 0:DQ].astype(F32)
        squares = jnp.sum(value * value, axis=1, keepdims=True)
        scaled = (value * gain_ref[j, 0:1, 0:DQ]).astype(BF16)
        part = jnp.dot(scaled, w1[pl.ds(mul(j * DQ, 16), DQ), :], preferred_element_type=F32)
        pre[:, 0:HD] = part if k == 0 else pre[:, 0:HD] + part
        transpose_chunk(1, j, True)
        return squares

    arrived([cot_cross])
    cot_far = send(cot.at[tp_cross], cot.at[tp_cross], sib)
    act_chunk(0)
    arrived([cot_sib])
    act_chunk(1)
    act_chunk(2)
    arrived([pos_cross])
    pos_far = send(pos.at[tp_cross], pos.at[tp_cross], sib)
    arrived([cot_far])
    act_chunk(3)

    own_half = pl.ds(mul(core * HQ, 16), HQ)

    def lanes_of(z_index):
        return pl.ds(mul(z_index * TOK, 128), TOK)

    def spread_a(g):
        copies = []
        for d in (1, 2, 3):
            target = (z + d) % 4
            copies.append(send(trans.at[g, target, own_half], at.at[g, y, own_half, lanes_of(z)], at_z(d)))
        own = local(trans.at[g, z, own_half], at.at[g, y, own_half, lanes_of(z)])
        return copies, own

    def spread_b(g):
        copies = []
        for d in (1, 2, 3):
            target = (y + d) % 4
            rows = pl.ds(mul(target * HQ, 16), HQ)
            copies.append(send(bt.at[g, rows], btile.at[g, y, :, lanes_of(z)], at_y(d)))
        rows = pl.ds(mul(y * HQ, 16), HQ)
        own = local(bt.at[g, rows], btile.at[g, y, :, lanes_of(z)])
        return copies, own

    def gather_a(g, spread):
        arrived(spread[0])
        spread[1].wait()
        block = at.at[g, y, own_half]
        copies = [send(block, block, at_y(d)) for d in (1, 3, 2)]
        return copies, [send(block, block, sib)]

    def share_a(g, gathered):
        for d, copy in zip((1, 3, 2), gathered[0]):
            copy.wait_recv()
            block = at.at[g, (y - d + 4) % 4, own_half]
            gathered[1].append(send(block, block, sib))

    def gather_b(g, spread):
        arrived(spread[0])
        spread[1].wait()
        block = btile.at[g, :, :, lanes_of(z)]
        return [send(block, block, at_z(d)) for d in (1, 3, 2)]

    spread_cot = spread_a(0)
    squares = pre_chunk(0)
    arrived([pos_sib])
    squares = squares + pre_chunk(1)
    squares = squares + pre_chunk(2)
    gather_cot = gather_a(0, spread_cot)
    arrived([pos_far])
    squares = squares + pre_chunk(3)
    inv[...] = jnp.broadcast_to(lax.rsqrt(squares * (1.0 / D) + epsilon), (TOK, 128))

    spread_pos = spread_a(1)

    def gelu_tile(k, total):
        lanes = pl.ds(mul(k * 128, 128), 128)
        raw = pre[:, lanes]
        scale = inv[...]
        value = raw * scale
        cdf = 0.5 * (1.0 + lax.erf(value * 0.7071067811865476))
        density = jnp.exp(-0.5 * value * value) * 0.3989422804014327
        slope = (dact[:, lanes] * (cdf + value * density) * scale).astype(BF16)
        b1[:, lanes] = slope
        slope = slope.astype(F32)
        bt[0, lanes, :] = (value * cdf).T.astype(BF16)
        bt[1, lanes, :] = slope.T.astype(BF16)
        return total + slope * raw

    inner = lax.fori_loop(0, 13, gelu_tile, jnp.zeros((TOK, 128), F32))
    spread_act = spread_b(0)
    spread_pre = spread_b(1)
    inn[tp] = jnp.broadcast_to(jnp.sum(inner.T, axis=0, keepdims=True), (8, 128))
    inner_copies = [send(inn.at[tp], inn.at[tp], to) for to in (sib, cross, far)]

    def norm_chunk(j):
        part = lax.dot_general(
            b1[:, 0:HD], w1[pl.ds(mul(j * DQ, 16), DQ), :], NT, preferred_element_type=F32
        )
        return part.astype(BF16)

    e_copies = []
    for k, (j, to) in enumerate(((tp_far, far), (tp_cross, cross), (tp_sib, sib))):
        e_send[k] = norm_chunk(j)
        e_copies.append(send(e_send.at[k], e_recv.at[tp], to))
        if k == 0:
            gather_act = gather_b(0, spread_act)
        if k == 1:
            gather_pre = gather_b(1, spread_pre)
    e_recv[tp] = norm_chunk(tp)
    gather_pos = gather_a(1, spread_pos)
    share_a(0, gather_cot)

    arrived(inner_copies)
    arrived(e_copies)
    inner_row = inn[0] + inn[1] + inn[2] + inn[3]
    factor = inv[...] * inv[...] * (1.0 / D)
    inv[...] = jnp.broadcast_to(inner_row[0:1, :], (TOK, 128)).T * factor

    def hidden_row(i, total):
        rows = pl.ds(mul(i * COLS, 16), COLS)
        e = e_recv[0, rows, :].astype(F32) + e_recv[1, rows, :].astype(F32)
        e = e + e_recv[2, rows, :].astype(F32) + e_recv[3, rows, :].astype(F32)
        h = pos[tp, rows, 0:DQ].astype(F32)
        d = cot[tp, rows, 0:DQ].astype(F32) + gain_ref[tp, 0:1, 0:DQ] * e - h * inv[rows, 0:1]
        padded2[i + 1, 8:24, :] = d.astype(BF16).astype(F32)
        return total + e * h

    gain_sum = lax.fori_loop(0, ROWS, hidden_row, jnp.zeros((COLS, DQ), F32))
    fill_edges(padded2, 1)
    halo2 = send_edges(1)

    kall[0, y] = jnp.zeros((16, DQ), F32)
    kall[0, y, 9:10, :] = jnp.sum(gain_sum, axis=0, keepdims=True)
    for n in range(7):
        lanes = slice(n * 128, min(n * 128 + 128, DQ))
        width = lanes.stop - lanes.start

        def taps(i, totals, lanes=lanes):
            d = padded2[i + 1, 8:24, lanes]
            return tuple(
                totals[p * 3 + q] + d * padded[i + p, 7 + q : 23 + q, lanes] for p in range(3) for q in range(3)
            )

        sums = lax.fori_loop(0, ROWS, taps, tuple(jnp.zeros((COLS, width), F32) for _ in range(9)))
        for k in range(9):
            kall[0, y, k : k + 1, lanes] = jnp.sum(sums[k], axis=0, keepdims=True)
    k_copies = [send(kall.at[0, y], kall.at[0, y], at_y(d)) for d in (1, 2, 3)]

    arrived(halo2)
    fill_halo(padded2, 1)

    def back_row(i, carry):
        total = padded2[i + 1, 8:24, :]
        for p in range(3):
            for q in range(3):
                total = total + pk_ref[tp, p * 3 + q : p * 3 + q + 1, :] * padded2[i + 2 - p, 9 - q : 25 - q, :]
        gt_ref[i] = total.astype(BF16)
        return carry

    lax.fori_loop(0, ROWS, back_row, 0)
    arrived(k_copies)
    kall[1, z] = kall[0, 0] + kall[0, 1] + kall[0, 2] + kall[0, 3]
    k_copies = [send(kall.at[1, z], kall.at[1, z], at_z(d)) for d in (1, 2, 3)]

    s = float(TOK * 32) ** -0.5

    def half(g, which):
        rows = pl.ds(mul(which * HQ, 16), HQ)
        total = lax.dot_general(at[g, 0, rows, :], btile[g, 0], NT, preferred_element_type=F32)
        for k in range(1, 4):
            total = total + lax.dot_general(at[g, k, rows, :], btile[g, k], NT, preferred_element_type=F32)
        return total * s

    def product(g, gathered_a, gathered_b):
        arrived(gathered_a[1])
        arrived(gathered_b)
        xs[g] = half(g, 1 - xh).astype(BF16)
        copy = send(xs.at[g], xr.at[g], x_peer)
        keep[g] = half(g, xh)
        return copy

    def turn(g, copy):
        copy.wait_recv()
        for k in range(4):
            rows = slice(k * 100, k * 100 + 100)
            ys[g, k, 0:100, :] = (keep[g, rows, :] + xr[g, rows, :].astype(F32)).astype(BF16)
        own = local(ys.at[g, y], yr.at[g, y])
        return [send(ys.at[g, (y + d) % 4], yr.at[g, y], at_y(d)) for d in (1, 3, 2)], own

    def finish(g, turned, out_ref):
        arrived(turned[0])
        turned[1].wait()
        for k in range(4):
            out_ref[:, k * HQ : (k + 1) * HQ] = yr[g, k, 0:100, :].astype(F32)

    x_copy0 = product(0, gather_cot, gather_act)
    arrived(k_copies)
    kall[2, xh] = kall[1, 0] + kall[1, 1] + kall[1, 2] + kall[1, 3]
    k_copy = send(kall.at[2, xh], kall.at[2, xh], x_peer)
    share_a(1, gather_pos)
    turn0 = turn(0, x_copy0)
    arrived([k_copy])
    kg_ref[...] = (kall[2, 0] + kall[2, 1]) * s
    x_copy1 = product(1, gather_pos, gather_pre)
    finish(0, turn0, gr_ref)
    turn1 = turn(1, x_copy1)
    finish(1, turn1, ge_ref)
    for copy in started:
        copy.wait_send()


def on_device(tokens, cotangent, expand_weight, reduce_weight, position_kernel, norm_gain):
    kernels = position_kernel.reshape(9, 4, DQ).transpose(1, 0, 2)
    gains = jnp.pad(norm_gain.reshape(4, 1, DQ), ((0, 0), (0, 0), (0, 96)))
    vmem = pl.BlockSpec(memory_space=pltpu.VMEM)
    hbm = pl.BlockSpec(memory_space=pl.ANY)
    f32, bf16 = (lambda *s: pltpu.VMEM(s, F32)), (lambda *s: pltpu.VMEM(s, BF16))
    grad_tokens, grad_expand, grad_reduce, small = pl.pallas_call(
        kernel,
        out_shape=(
            jax.ShapeDtypeStruct((ROWS, COLS, DQ), BF16),
            jax.ShapeDtypeStruct((100, HD), F32),
            jax.ShapeDtypeStruct((100, HD), F32),
            jax.ShapeDtypeStruct((16, DQ), F32),
        ),
        in_specs=[vmem, vmem, hbm, hbm, vmem, vmem],
        out_specs=(vmem, vmem, vmem, vmem),
        scratch_shapes=[
            bf16(D, HD), bf16(D, HD),
            f32(10, 32, DQ), f32(10, 32, DQ),
            bf16(4, TOK, 896), bf16(4, TOK, 896),
            bf16(2, 4, 896, TOK),
            f32(TOK, HP), f32(TOK, HP),
            f32(TOK, 128),
            bf16(2, HP, TOK), bf16(TOK, HP),
            bf16(2, 4, DQ, 512), bf16(2, 4, HQ, 512),
            bf16(3, TOK, DQ), bf16(4, TOK, DQ),
            f32(4, 8, 128),
            f32(2, 2, 16, DQ), f32(2, 2, 8, DQ),
            f32(2, 2, 16, DQ), f32(2, 2, 8, DQ), f32(2, 4, 8, DQ),
            bf16(2, HQ, HQ), bf16(2, HQ, HQ), f32(2, HQ, HQ),
            bf16(2, 4, 112, HQ), bf16(2, 4, 112, HQ),
            f32(3, 4, 16, DQ),
            pltpu.SemaphoreType.DMA((96,)), pltpu.SemaphoreType.DMA((96,)),
            pltpu.SemaphoreType.DMA((8,)), pltpu.SemaphoreType.DMA((8,)),
        ],
        compiler_params=pltpu.CompilerParams(
            collective_id=0, has_side_effects=True, vmem_limit_bytes=60 * 2**20
        ),
        name="mlp_backward",
    )(tokens, cotangent, expand_weight, reduce_weight, kernels, gains)
    return grad_tokens, grad_expand, grad_reduce, small[0:9].reshape(3, 3, DQ), small[9]


def solution(mesh):
    placed = (P("row", "col", "tp"), P("row", "col", "tp"), P(None, "tp"), P(None, "tp"), P(), P())
    return jax.shard_map(
        on_device,
        mesh=mesh,
        in_specs=placed,
        out_specs=(
            P("row", "col", "tp"),
            P(("row", "col"), "tp"),
            P(("row", "col"), "tp"),
            P(None, None, "tp"),
            P("tp"),
        ),
        check_vma=False,
    )
```

time: 675 us -> 167 us (0.25)
  waiting for transfers between devices: 274 us -> 0 us
  blocking collectives: 264 us -> 0 us
  Pallas kernels: 0 us -> 121 us
  other arithmetic: 28 us -> 0 us
  matrix products: 23.8 us -> 0 us
  starting transfers between devices: 23 us -> 0 us
  between operations: 16.8 us -> 0.65 us
    ppermute x8 -> x0, waiting for transfers between devices: 214 us -> none  [the longest x4 213 us: padded_2(): lax.ppermute(tail, axis, [(i, (i + 1) % count) for i in range(ends)])]
    psum x2 -> x0, blocking collectives: 183 us -> none  [the longest x1 177 us: on_device(): lax.psum((local_gain, local_kernel), ('row', 'col'))]
    pallas_call x0 -> x1, Pallas kernels: none -> 121 us  [on_device(): pl.pallas_call(kernel, out_shape=(jax.ShapeDtypeStruct((ROWS, COLS, DQ),...]
    all_gather x2 -> x0, blocking collectives: 81.2 us -> none  [the longest x1 40.8 us: on_device(): lax.all_gather(own_h, 'tp', axis=2, tiled=True)]
    unnamed x4 -> x0, waiting for transfers between devices: 60.8 us -> none
    dot_general x5 -> x0, matrix products: 23.8 us -> none  [the longest x1 7 us: on_device(): lax.dot_general(flat_cot, activated, (((0,), (0,)), ((), ())), preferred_...]
    ppermute x8 -> x0, starting transfers between devices: 22.7 us -> none  [the longest x4 17.6 us: padded_2(): lax.ppermute(tail, axis, [(i, (i + 1) % count) for i in range(ends)])]
    concatenate x1 -> x0, other arithmetic: 21.7 us -> none  [on_device(): jnp.concatenate([lax.dot_general(normed, d_pre, (((0,), (0,)), ((), ())),...]
  transfers between devices with their start and end apart: 10 -> 0, of which waited for: 3 -> 0; matrix products, arithmetic and copies ran while one was open for 6% -> 0% of each run, Pallas kernels for 0% -> 0%
where the time goes in v1:
time: 167 us; the launch traced here: 166 us
  Pallas kernels  121 us (72%)
  local copies, waits for them, and re-layouts  44.8 us (27%)
    pallas_call x1, Pallas kernels, on_device(): pl.pallas_call(kernel, out_shape=(jax.ShapeDtypeStruct((ROWS, COLS, DQ),...  121 us
    unnamed x5, local copies, waits for them, and re-layouts  38.8 us

profile of v1, /device:TPU:0, one launch (start us, length us, event | category | flops | bytes accessed | tf_op | source)
XLA Modules:
  0.0 166.0 jit_solution(15682993438546483275)
XLA Ops:
  0.6 0.8 reshape.20
  1.4 0.6 pad.4.gain_ref
  2.0 1.1 reshape.19
  3.1 0.7 copy.17
  3.8 16.3 %copy.14.w1_hbm = bf16[3200,1600]{1,0:T(8,128)(2,1)} copy(bf16[3200,1600]{0,1:T(8,128)(2,1)} %param.8) | data formatting | bytes 20480000 | tf_op args[2]
  20.2 16.8 %copy.15.w2_hbm = bf16[3200,1600]{1,0:T(8,128)(2,1)} copy(bf16[3200,1600]{0,1:T(8,128)(2,1)} %param.9) | data formatting | bytes 20480000 | tf_op args[3]
  37.0 120.6 %mlp_backward.1 = (bf16[8,16,800]{2,1,0:T(8,128)(2,1)}, f32[100,1600]{1,0:T(8,128)}, f32[100,1600]{1,0:T(8,128)}, f32[16,800]{1,0:T(8,128)}) custom-call(bf16[8,16,800]{2,1,0:T(8,128)(2,1)} %tok_ref.1, bf16[8,16,800]{2,1,0:T(8,128)(2,1)} %cot_ref.1, bf16[3200,1600]{1,0:T(8,128)(2,1)} %copy.14.w1_hbm, bf16[3200,1600]{1,0:T(8,128)(2,1)} %copy.15.w2_hbm, ...), custom_call_target="tpu_custom_call" | custom-call | tf_op jit(solution)/shard_map/mlp_backward/pallas_call | solution.py:394
  157.6 1.4 slice_reduce_fusion
  158.9 1.5 reshape.21
  160.4 1.6 copy.21
  162.0 2.0 %copy.22 = f32[100,1600]{1,0:T(8,128)} copy(f32[100,1600]{1,0:T(8,128)} %get-tuple-element.19) | data formatting | bytes 1280000
  164.0 2.0 %copy.23 = f32[100,1600]{1,0:T(8,128)} copy(f32[100,1600]{1,0:T(8,128)} %get-tuple-element.20) | data formatting | bytes 1280000

commit v2 on v1

v2 whole, which is shorter than its diff:
```python
import jax
import jax.numpy as jnp
from jax import lax
from jax.experimental import pallas as pl
from jax.experimental.pallas import tpu as pltpu
from jax.sharding import PartitionSpec as P

MESH = pl.DeviceIdType.MESH
F32 = jnp.float32
BF16 = jnp.bfloat16
epsilon = 1e-06
ROWS, COLS, TOK = 8, 16, 128
DQ, D, FR = 800, 3200, 896
HD, HQ = 1600, 400
NT = (((1,), (1,)), ((), ()))
PARTS = ((0, 0, 400), (1, 0, 256), (1, 256, 144))


def mul(value, by):
    return pl.multiple_of(value, by)


def kernel(
    tok_ref, cot_ref, w1_hbm, w2_hbm, pk_ref, gain_ref,
    gt_ref, yr0, yr1, yr2, kg_ref,
    w1, w2, padded, padded2, cot, pos, trans, pre, dact, inv, bt, b1, at, btile,
    e_send, e_recv, inn, erow, ecol, rrow, rcol, rcor,
    xs0, xs1, xs2, xr0, xr1, xr2, keep0, keep1, keep2, ys0, ys1, ys2, kall,
    send_sem, recv_sem, local_sem, wsem,
):
    z = lax.axis_index("row")
    col = lax.axis_index("col")
    tp = lax.axis_index("tp")
    xh, y = col // 4, col % 4
    xl, core = tp // 2, tp % 2

    def at_y(d):
        return (z, xh * 4 + (y + d) % 4, tp)

    def at_z(d):
        return ((z + d) % 4, col, tp)

    def at_grid(dr, dc):
        return ((z + dr + 4) % 4, (col + dc + 8) % 8, tp)

    x_peer = (z, (1 - xh) * 4 + y, tp)
    tp_sib = xl * 2 + 1 - core
    tp_cross = (1 - xl) * 2 + core
    tp_far = (1 - xl) * 2 + 1 - core
    sib, cross, far = (z, col, tp_sib), (z, col, tp_cross), (z, col, tp_far)

    w_copies = []
    for n, (src, dst) in enumerate(((w2_hbm, w2), (w1_hbm, w1))):
        for k in range(4):
            rows = pl.ds(k * HQ, HQ)
            copy = pltpu.make_async_copy(src.at[rows], dst.at[rows], wsem.at[n * 4 + k])
            copy.start()
            w_copies.append(copy)

    for g in range(2):
        for j in range(4):
            trans[g, j, 0:96, :] = jnp.zeros((96, TOK), BF16)
            trans[g, j, 800:896, :] = jnp.zeros((96, TOK), BF16)

    grid_steps = [(1, 0), (-1, 0), (0, 1), (0, -1), (1, 1), (1, -1), (-1, 1), (-1, -1)]
    peers = [at_grid(*s) for s in grid_steps]
    peers += [at_y(d) for d in (1, 2, 3)] + [at_z(d) for d in (1, 2, 3)]
    peers += [x_peer, sib, cross, far]
    barrier = pltpu.get_barrier_semaphore()
    for peer in peers:
        pl.semaphore_signal(barrier, inc=1, device_id=peer, device_id_type=MESH)

    counts = {"remote": 0, "local": 0}
    started = []

    def send(src, dst, to):
        k = counts["remote"]
        counts["remote"] += 1
        copy = pltpu.make_async_remote_copy(
            src_ref=src, dst_ref=dst, send_sem=send_sem.at[k], recv_sem=recv_sem.at[k],
            device_id=to, device_id_type=MESH,
        )
        copy.start()
        started.append(copy)
        return copy

    def local(src, dst):
        k = counts["local"]
        counts["local"] += 1
        copy = pltpu.make_async_copy(src, dst, local_sem.at[k])
        copy.start()
        return copy

    def arrived(copies):
        for copy in copies:
            copy.wait_recv()

    def fill_edges(field, n):
        erow[n, 0] = field[1, 8:24, :]
        erow[n, 1] = field[8, 8:24, :]
        for i in range(ROWS):
            ecol[n, 0, i : i + 1, :] = field[i + 1, 8:9, :]
            ecol[n, 1, i : i + 1, :] = field[i + 1, 23:24, :]

    def send_edges(n):
        low, high = pl.ds(0, 8), pl.ds(8, 8)
        return [
            send(erow.at[n, 1], rrow.at[n, 0], at_grid(1, 0)),
            send(erow.at[n, 0], rrow.at[n, 1], at_grid(-1, 0)),
            send(ecol.at[n, 1], rcol.at[n, 0], at_grid(0, 1)),
            send(ecol.at[n, 0], rcol.at[n, 1], at_grid(0, -1)),
            send(erow.at[n, 1, high], rcor.at[n, 0], at_grid(1, 1)),
            send(erow.at[n, 1, low], rcor.at[n, 1], at_grid(1, -1)),
            send(erow.at[n, 0, high], rcor.at[n, 2], at_grid(-1, 1)),
            send(erow.at[n, 0, low], rcor.at[n, 3], at_grid(-1, -1)),
        ]

    one, zero = jnp.float32(1), jnp.float32(0)
    top = jnp.where(z > 0, one, zero)
    bottom = jnp.where(z < 3, one, zero)
    left = jnp.where(col > 0, one, zero)
    right = jnp.where(col < 7, one, zero)

    def fill_halo(field, n):
        field[0, 8:24, :] = rrow[n, 0] * top
        field[9, 8:24, :] = rrow[n, 1] * bottom
        for i in range(ROWS):
            field[i + 1, 7:8, :] = rcol[n, 0, i : i + 1, :] * left
            field[i + 1, 24:25, :] = rcol[n, 1, i : i + 1, :] * right
        field[0, 7:8, :] = rcor[n, 0, 7:8, :] * (top * left)
        field[0, 24:25, :] = rcor[n, 1, 0:1, :] * (top * right)
        field[9, 7:8, :] = rcor[n, 2, 7:8, :] * (bottom * left)
        field[9, 24:25, :] = rcor[n, 3, 0:1, :] * (bottom * right)

    shift = tp * 32
    frame = pl.ds(mul(tp * 768, 128), FR)
    filled = pl.ds(mul(tp * 32, 16), DQ)

    def to_frame(field, i, values):
        field[i + 1, 8:24, 768:896] = jnp.zeros((COLS, 128), F32)
        field[i + 1, 8:24, 0:DQ] = values.astype(F32)
        return pltpu.roll(field[i + 1, 8:24, :], shift, 1)

    for i in range(ROWS):
        padded[i + 1, 8:24, :] = to_frame(padded, i, tok_ref[i])
    fill_edges(padded, 0)
    pl.semaphore_wait(barrier, len(peers))
    halo = send_edges(0)
    for i in range(ROWS):
        cot[i * COLS : (i + 1) * COLS, :] = to_frame(padded2, i, cot_ref[i]).astype(BF16)

    def own_transpose(g, source):
        for k in range(7):
            trans[g, tp, k * 128 : k * 128 + 128, :] = source[:, k * 128 : k * 128 + 128].T

    def send_chunk(g, j, to):
        rows = pl.ds(mul(j * 32, 16), DQ)
        return send(trans.at[g, j, rows], trans.at[g, j, rows], to)

    own_transpose(0, cot)
    cot_cross = send_chunk(0, tp, cross)
    cot_sib = send_chunk(0, tp, sib)

    arrived(halo)
    fill_halo(padded, 0)

    def conv_row(i, squares):
        total = padded[i + 1, 8:24, :]
        for p in range(3):
            for q in range(3):
                total = total + pk_ref[p, q : q + 1, frame] * padded[i + p, 7 + q : 23 + q, :]
        rows = pl.ds(mul(i * COLS, 16), COLS)
        total = total.astype(BF16)
        pos[rows, :] = total
        total = total.astype(F32)
        b1[rows, 0:FR] = (total * gain_ref[0:1, frame]).astype(BF16)
        inv[rows, :] = jnp.broadcast_to(jnp.sum(total * total, axis=1, keepdims=True), (COLS, TOK))
        return squares

    lax.fori_loop(0, ROWS, conv_row, 0)
    own_transpose(1, b1)
    pos_cross = send_chunk(1, tp, cross)
    pos_sib = send_chunk(1, tp, sib)
    inn[0, tp] = inv[...].T[0:8, :]
    square_copies = [send(inn.at[0, tp], inn.at[0, tp], to) for to in (sib, cross, far)]

    def product_chunk(g, j, first):
        total, weight = (pre, w1) if g else (dact, w2)
        part = jnp.dot(weight[:, pl.ds(mul(j * 768, 128), FR)], trans[g, j], preferred_element_type=F32)
        total[...] = part if first else total[...] + part

    own_half = pl.ds(mul(core * HQ, 16), HQ)

    def lanes_of(z_index):
        return pl.ds(mul(z_index * TOK, 128), TOK)

    def half_of(j):
        return pl.ds(mul(j * 32 + core * HQ, 16), HQ)

    def spread_a(g):
        copies = []
        for d in (1, 2, 3):
            target = (z + d) % 4
            copies.append(
                send(trans.at[g, target, half_of(target)], at.at[g, y, own_half, lanes_of(z)], at_z(d))
            )
        return copies, local(trans.at[g, z, half_of(z)], at.at[g, y, own_half, lanes_of(z)])

    def spread_b(part):
        g, first, count = PARTS[part]
        copies = []
        for d in (1, 2, 3):
            rows = pl.ds(mul((y + d) % 4 * HQ + first, 16), count)
            copies.append(
                send(bt.at[g, rows], btile.at[g, y, pl.ds(first, count), lanes_of(z)], at_y(d))
            )
        rows = pl.ds(mul(y * HQ + first, 16), count)
        return copies, local(bt.at[g, rows], btile.at[g, y, pl.ds(first, count), lanes_of(z)])

    class Gather:
        def __init__(self, spread, block, piece, to, me, share):
            arrived(spread[0])
            spread[1].wait()
            self.block, self.piece, self.to, self.me, self.share = block, piece, to, me, share
            self.shared = []
            own = block(me)
            self.up, self.down = send(own, own, to(1)), send(own, own, to(3))
            self.to_sibling(own)

        def to_sibling(self, ref):
            if self.share:
                self.shared.append(send(ref, ref, sib))

        def forward(self):
            below, above = (self.me + 3) % 4, (self.me + 1) % 4
            self.up.wait_recv()
            first = self.piece(below, 0)
            self.up = send(first, first, self.to(1))
            self.down.wait_recv()
            second = self.piece(above, 1)
            self.down = send(second, second, self.to(3))
            self.to_sibling(self.block(below))
            self.to_sibling(self.block(above))

        def end(self):
            self.up.wait_recv()
            self.down.wait_recv()
            self.to_sibling(self.block((self.me + 2) % 4))

        def ready(self):
            arrived(self.shared)

    def gather_a(g, spread):
        def block(i):
            return at.at[g, i, own_half]

        def piece(i, h):
            return at.at[g, i, own_half, pl.ds(h * 256, 256)]

        return Gather(spread, block, piece, at_y, y, True)

    def gather_b(part, spread):
        g, first, count = PARTS[part]

        def block(i):
            return btile.at[g, :, pl.ds(first, count), lanes_of(i)]

        def piece(i, h):
            return btile.at[g, pl.ds(h * 2, 2), pl.ds(first, count), lanes_of(i)]

        return Gather(spread, block, piece, at_z, z, False)

    arrived([cot_cross])
    cot_far = send_chunk(0, tp_cross, sib)
    for copy in w_copies[:4]:
        copy.wait()
    product_chunk(0, tp, True)
    arrived([cot_sib])
    product_chunk(0, tp_sib, False)
    arrived([cot_far])
    spread_cot = spread_a(0)
    product_chunk(0, tp_cross, False)
    product_chunk(0, tp_far, False)
    for copy in w_copies[4:]:
        copy.wait()
    product_chunk(1, tp, True)
    arrived([pos_cross])
    pos_far = send_chunk(1, tp_cross, sib)
    arrived([pos_sib])
    product_chunk(1, tp_sib, False)
    product_chunk(1, tp_cross, False)
    gather_cot = gather_a(0, spread_cot)
    arrived([pos_far])
    spread_pos = spread_a(1)
    product_chunk(1, tp_far, False)
    arrived(square_copies)
    squares = inn[0, 0] + inn[0, 1] + inn[0, 2] + inn[0, 3]
    row_inv = lax.rsqrt(squares[0:1, :] * (1.0 / D) + epsilon)

    def gelu_tile(k, total):
        rows = pl.ds(mul(k * 64, 16), 64)
        raw = pre[rows, :]
        value = raw * row_inv
        cdf = 0.5 * (1.0 + lax.erf(value * 0.7071067811865476))
        density = jnp.exp(-0.5 * value * value) * 0.3989422804014327
        slope = (dact[rows, :] * (cdf + value * density) * row_inv).astype(BF16)
        bt[0, rows, :] = (value * cdf).astype(BF16)
        bt[1, rows, :] = slope
        return total + jnp.sum(slope.astype(F32) * raw, axis=0, keepdims=True)

    inner = lax.fori_loop(0, 25, gelu_tile, jnp.zeros((1, TOK), F32))
    spread_act = spread_b(0)
    inn[1, tp] = jnp.broadcast_to(inner, (8, TOK))
    inner_copies = [send(inn.at[1, tp], inn.at[1, tp], to) for to in (sib, cross, far)]

    for k in range(12):
        b1[:, k * 128 : k * 128 + 128] = bt[1, k * 128 : k * 128 + 128, :].T
    b1[:, 1536:1600] = bt[1, 1536:1600, :].T

    def norm_chunk(j):
        part = jnp.dot(b1[...], w1[:, pl.ds(mul(j * 768, 128), FR)], preferred_element_type=F32)
        return part.astype(BF16)

    e_copies = []
    for k, (j, to) in enumerate(((tp_far, far), (tp_cross, cross), (tp_sib, sib))):
        e_send[k] = norm_chunk(j)
        e_copies.append(send(e_send.at[k], e_recv.at[tp], to))
    e_recv[tp] = norm_chunk(tp)
    gather_act = gather_b(0, spread_act)
    spread_pre = [spread_b(1), spread_b(2)]
    gather_cot.forward()
    gather_pos = gather_a(1, spread_pos)

    arrived(inner_copies)
    arrived(e_copies)
    inner_row = inn[1, 0] + inn[1, 1] + inn[1, 2] + inn[1, 3]
    factor = inner_row[0:1, :] * row_inv * row_inv * (1.0 / D)
    inv[...] = jnp.broadcast_to(factor, (TOK, TOK)).T

    def hidden_row(i, total):
        rows = pl.ds(mul(i * COLS, 16), COLS)
        e = e_recv[0, rows, :].astype(F32) + e_recv[1, rows, :].astype(F32)
        e = e + e_recv[2, rows, :].astype(F32) + e_recv[3, rows, :].astype(F32)
        h = pos[rows, :].astype(F32)
        d = cot[rows, :].astype(F32) + gain_ref[0:1, frame] * e - h * inv[rows, 0:1]
        padded2[i + 1, 8:24, :] = d.astype(BF16).astype(F32)
        return total + e * h

    gain_sum = lax.fori_loop(0, ROWS, hidden_row, jnp.zeros((COLS, FR), F32))
    fill_edges(padded2, 1)
    halo2 = send_edges(1)
    gather_act.forward()
    gather_pre = [gather_b(1, spread_pre[0]), gather_b(2, spread_pre[1])]

    kall[0, y] = jnp.zeros((16, FR), F32)
    kall[0, y, 9:10, :] = jnp.sum(gain_sum, axis=0, keepdims=True)
    for n in range(7):
        lanes = slice(n * 128, n * 128 + 128)

        def taps(i, totals, lanes=lanes):
            d = padded2[i + 1, 8:24, lanes]
            return tuple(
                totals[p * 3 + q] + d * padded[i + p, 7 + q : 23 + q, lanes] for p in range(3) for q in range(3)
            )

        sums = lax.fori_loop(0, ROWS, taps, tuple(jnp.zeros((COLS, 128), F32) for _ in range(9)))
        for k in range(9):
            kall[0, y, k : k + 1, lanes] = jnp.sum(sums[k], axis=0, keepdims=True)
    k_copies = [send(kall.at[0, y], kall.at[0, y], at_y(d)) for d in (1, 2, 3)]

    arrived(halo2)
    fill_halo(padded2, 1)
    unshift = FR - shift

    def back_row(i, carry):
        total = padded2[i + 1, 8:24, :]
        for p in range(3):
            for q in range(3):
                total = total + pk_ref[p, q : q + 1, frame] * padded2[i + 2 - p, 9 - q : 25 - q, :]
        gt_ref[i] = pltpu.roll(total, unshift, 1)[:, 0:DQ].astype(BF16)
        return carry

    lax.fori_loop(0, ROWS, back_row, 0)
    arrived(k_copies)
    kall[1, z] = kall[0, 0] + kall[0, 1] + kall[0, 2] + kall[0, 3]
    k_copies = [send(kall.at[1, z], kall.at[1, z], at_z(d)) for d in (1, 2, 3)]

    s = float(TOK * 32) ** -0.5

    xs, xr, keep = (xs0, xs1, xs2), (xr0, xr1, xr2), (keep0, keep1, keep2)
    ys, yr = (ys0, ys1, ys2), (yr0, yr1, yr2)

    def half(part, which):
        g, first, count = PARTS[part]
        rows, hidden = pl.ds(mul(which * HQ, 16), HQ), pl.ds(first, count)
        total = lax.dot_general(at[g, 0, rows, :], btile[g, 0, hidden, :], NT, preferred_element_type=F32)
        for k in range(1, 4):
            total = total + lax.dot_general(
                at[g, k, rows, :], btile[g, k, hidden, :], NT, preferred_element_type=F32
            )
        return total * s

    def product(part):
        xs[part][...] = half(part, 1 - xh).astype(BF16)
        copy = send(xs[part], xr[part], x_peer)
        keep[part][...] = half(part, xh)
        return copy

    def turn(part, copy):
        copy.wait_recv()
        for k in range(4):
            rows = slice(k * 100, k * 100 + 100)
            ys[part][k, 0:100, :] = (keep[part][rows, :] + xr[part][rows, :].astype(F32)).astype(BF16)
        own = local(ys[part].at[y], yr[part].at[y])
        return [send(ys[part].at[(y + d) % 4], yr[part].at[y], at_y(d)) for d in (1, 3, 2)], own

    gather_cot.end()
    gather_act.end()
    gather_cot.ready()
    x_copy0 = product(0)
    gather_pos.forward()
    for gather in gather_pre:
        gather.forward()
    arrived(k_copies)
    kall[2, xh] = kall[1, 0] + kall[1, 1] + kall[1, 2] + kall[1, 3]
    k_copy = send(kall.at[2, xh], kall.at[2, xh], x_peer)
    turns = [turn(0, x_copy0)]
    gather_pos.end()
    arrived([k_copy])
    kg_ref[...] = pltpu.roll((kall[2, 0] + kall[2, 1]) * s, unshift, 1)
    gather_pos.ready()
    gather_pre[0].end()
    x_copy1 = product(1)
    gather_pre[1].end()
    x_copy2 = product(2)
    turns.append(turn(1, x_copy1))
    turns.append(turn(2, x_copy2))
    for copies, own in turns:
        arrived(copies)
        own.wait()
    for copy in started:
        copy.wait_send()


def finish(gt_in, part0, part1, part2, small, gt_ref, ge_ref, gr_ref, gk_ref, gg_ref):
    gt_ref[...] = gt_in[...]
    for (g, first, count), part in zip(PARTS, (part0, part1, part2)):
        out = ge_ref if g else gr_ref
        for k in range(4):
            out[:, k * HQ + first : k * HQ + first + count] = part[k, 0:100, :].astype(F32)
    for p in range(3):
        gk_ref[p] = small[3 * p : 3 * p + 3, 0:DQ]
    gg_ref[...] = small[9:10, 0:DQ]


def on_device(tokens, cotangent, expand_weight, reduce_weight, position_kernel, norm_gain):
    vmem = pl.BlockSpec(memory_space=pltpu.VMEM)
    hbm = pl.BlockSpec(memory_space=pl.ANY)
    f32, bf16 = (lambda *s: pltpu.VMEM(s, F32)), (lambda *s: pltpu.VMEM(s, BF16))
    gt, part0, part1, part2, small = pl.pallas_call(
        kernel,
        out_shape=(
            jax.ShapeDtypeStruct((ROWS, COLS, DQ), BF16),
            *[jax.ShapeDtypeStruct((4, 112, n), BF16) for _, _, n in PARTS],
            jax.ShapeDtypeStruct((16, FR), F32),
        ),
        in_specs=[vmem, vmem, hbm, hbm, vmem, vmem],
        out_specs=(vmem,) * 5,
        scratch_shapes=[
            bf16(HD, D), bf16(HD, D),
            f32(10, 32, FR), f32(10, 32, FR),
            bf16(TOK, FR), bf16(TOK, FR),
            bf16(2, 4, FR, TOK),
            f32(HD, TOK), f32(HD, TOK),
            f32(TOK, TOK),
            bf16(2, HD, TOK), bf16(TOK, HD),
            bf16(2, 4, DQ, 512), bf16(2, 4, HQ, 512),
            bf16(3, TOK, FR), bf16(4, TOK, FR),
            f32(2, 4, 8, TOK),
            f32(2, 2, 16, FR), f32(2, 2, 8, FR),
            f32(2, 2, 16, FR), f32(2, 2, 8, FR), f32(2, 4, 8, FR),
            *[bf16(HQ, n) for _, _, n in PARTS],
            *[bf16(HQ, n) for _, _, n in PARTS],
            *[f32(HQ, n) for _, _, n in PARTS],
            *[bf16(4, 112, n) for _, _, n in PARTS],
            f32(3, 4, 16, FR),
            pltpu.SemaphoreType.DMA((112,)), pltpu.SemaphoreType.DMA((112,)),
            pltpu.SemaphoreType.DMA((8,)), pltpu.SemaphoreType.DMA((8,)),
        ],
        compiler_params=pltpu.CompilerParams(
            collective_id=0, has_side_effects=True, vmem_limit_bytes=60 * 2**20
        ),
        name="mlp_backward",
    )(tokens, cotangent, expand_weight.T, reduce_weight.T, position_kernel, norm_gain.reshape(1, D))
    grad_tokens, grad_expand, grad_reduce, grad_kernel, grad_gain = pl.pallas_call(
        finish,
        out_shape=(
            jax.ShapeDtypeStruct((ROWS, COLS, DQ), BF16),
            jax.ShapeDtypeStruct((100, HD), F32),
            jax.ShapeDtypeStruct((100, HD), F32),
            jax.ShapeDtypeStruct((3, 3, DQ), F32),
            jax.ShapeDtypeStruct((1, DQ), F32),
        ),
        in_specs=[vmem] * 5,
        out_specs=(vmem,) * 5,
        name="finish",
    )(gt, part0, part1, part2, small)
    return grad_tokens, grad_expand, grad_reduce, grad_kernel, grad_gain.reshape(DQ)


def solution(mesh):
    placed = (P("row", "col", "tp"), P("row", "col", "tp"), P(None, "tp"), P(None, "tp"), P(), P())
    return jax.shard_map(
        on_device,
        mesh=mesh,
        in_specs=placed,
        out_specs=(
            P("row", "col", "tp"),
            P(("row", "col"), "tp"),
            P(("row", "col"), "tp"),
            P(None, None, "tp"),
            P("tp"),
        ),
        check_vma=False,
    )
```

time: 167 us -> 105 us (0.63)
  local copies, waits for them, and re-layouts: 44.8 us -> 1.33 us
  Pallas kernels: 121 us -> 102 us
    unnamed x5 -> x0, local copies, waits for them, and re-layouts: 38.8 us -> none
    pallas_call x1, Pallas kernels: 121 us -> 98.9 us  [on_device(): pl.pallas_call(kernel, out_shape=(jax.ShapeDtypeStruct((ROWS, COLS, DQ),...]
    reshape x4 -> x1, local copies, waits for them, and re-layouts: 4.04 us -> 1.33 us  [on_device(): norm_gain.reshape(1, D)]
    pallas_call x0 -> x1, Pallas kernels: none -> 2.63 us  [on_device(): pl.pallas_call(finish, out_shape=(jax.ShapeDtypeStruct((ROWS, COLS, DQ),...]
where the time goes in v2:
time: 105 us
  Pallas kernels  102 us (97%)
  local copies, waits for them, and re-layouts  1.33 us (1%)
  other arithmetic  1.28 us (1%)
    pallas_call x1, Pallas kernels, on_device(): pl.pallas_call(kernel, out_shape=(jax.ShapeDtypeStruct((ROWS, COLS, DQ),...  98.9 us
    pallas_call x1, Pallas kernels, on_device(): pl.pallas_call(finish, out_shape=(jax.ShapeDtypeStruct((ROWS, COLS, DQ),...  2.63 us

profile of v2, /device:TPU:0, one launch (start us, length us, event | category | flops | bytes accessed | tf_op | source)
XLA Modules:
  0.0 104.8 jit_solution(12986280360494004668)
XLA Ops:
  0.6 1.3 %reshape.16.gain_ref = f32[1,3200]{1,0:T(1,128)} reshape(f32[3200]{0:T(1024)} %param.11) | data formatting | bytes 25600 | tf_op jit(solution)/shard_map/reshape | solution.py:494
  2.0 98.9 %mlp_backward.1 = (bf16[8,16,800]{2,1,0:T(8,128)(2,1)}, bf16[4,112,400]{2,1,0:T(8,128)(2,1)}, bf16[4,112,256]{2,1,0:T(8,128)(2,1)}, bf16[4,112,144]{2,1,0:T(8,128)(2,1)}, f32[16,896]{1,0:T(8,128)}) custom-call(bf16[8,16,800]{2,1,0:T(8,128)(2,1)} %tok_ref.1, bf16[8,16,800]{2,1,0:T(8,128)(2,1)} %cot_ref.1, bf16[1600,3200]{1,0:T(8,128)(2,1)} %bitcast.2, ...), custom_call_target="tpu_custom_call" | custom-call | tf_op jit(solution)/shard_map/mlp_backward/pallas_call | solution.py:460
  100.9 2.6 %finish.1 = (bf16[8,16,800]{2,1,0:T(8,128)(2,1)}, f32[100,1600]{1,0:T(8,128)}, f32[100,1600]{1,0:T(8,128)}, f32[3,3,800]{2,1,0:T(4,128)}, f32[1,800]{1,0:T(1,128)}) custom-call(bf16[8,16,800]{2,1,0:T(8,128)(2,1)} %get-tuple-element.15.gt_in, bf16[4,112,400]{2,1,0:T(8,128)(2,1)} %get-tuple-element.16.part0, bf16[4,112,256]{2,1,0:T(8,128)(2,1)} %get-tuple-element.17.part1, ...), custom_call_target="tpu_custom_call" | custom-call | tf_op jit(solution)/shard_map/finish/pallas_call | solution.py:495
  103.5 1.3 %reduce = f32[800]{0:T(1024)} reduce(f32[1,800]{1,0:T(1,128)} %get-tuple-element.24, f32[]{:T(128)} %constant), dimensions={0}, to_apply=%get-tuple-element.24.reduce_sub_computation | reduce | bytes 6404 | tf_op jit(solution)/shard_map/finish/pallas_call | solution.py:495

commit v3 on v2

--- a/solution.py
+++ b/solution.py
@@ -23,7 +23,7 @@
 def kernel(
     tok_ref, cot_ref, w1_hbm, w2_hbm, pk_ref, gain_ref,
     gt_ref, yr0, yr1, yr2, kg_ref,
-    w1, w2, padded, padded2, cot, pos, trans, pre, dact, inv, bt, b1, at, btile,
+    w1, w2, gain, padded, padded2, cot, pos, trans, pre, dact, inv, bt, b1, at, btile,
     e_send, e_recv, inn, erow, ecol, rrow, rcol, rcor,
     xs0, xs1, xs2, xr0, xr1, xr2, keep0, keep1, keep2, ys0, ys1, ys2, kall,
     send_sem, recv_sem, local_sem, wsem,
@@ -56,6 +56,9 @@
             copy = pltpu.make_async_copy(src.at[rows], dst.at[rows], wsem.at[n * 4 + k])
             copy.start()
             w_copies.append(copy)
+
+    for k in range(25):
+        gain[0:1, k * 128 : k * 128 + 128] = gain_ref[k : k + 1, :]
 
     for g in range(2):
         for j in range(4):
@@ -173,7 +176,7 @@
         total = total.astype(BF16)
         pos[rows, :] = total
         total = total.astype(F32)
-        b1[rows, 0:FR] = (total * gain_ref[0:1, frame]).astype(BF16)
+        b1[rows, 0:FR] = (total * gain[0:1, frame]).astype(BF16)
         inv[rows, :] = jnp.broadcast_to(jnp.sum(total * total, axis=1, keepdims=True), (COLS, TOK))
         return squares
 
@@ -310,6 +313,7 @@
 
     inner = lax.fori_loop(0, 25, gelu_tile, jnp.zeros((1, TOK), F32))
     spread_act = spread_b(0)
+    spread_pre = [spread_b(1), spread_b(2)]
     inn[1, tp] = jnp.broadcast_to(inner, (8, TOK))
     inner_copies = [send(inn.at[1, tp], inn.at[1, tp], to) for to in (sib, cross, far)]
 
@@ -327,7 +331,6 @@
         e_copies.append(send(e_send.at[k], e_recv.at[tp], to))
     e_recv[tp] = norm_chunk(tp)
     gather_act = gather_b(0, spread_act)
-    spread_pre = [spread_b(1), spread_b(2)]
     gather_cot.forward()
     gather_pos = gather_a(1, spread_pos)
 
@@ -342,7 +345,7 @@
         e = e_recv[0, rows, :].astype(F32) + e_recv[1, rows, :].astype(F32)
         e = e + e_recv[2, rows, :].astype(F32) + e_recv[3, rows, :].astype(F32)
         h = pos[rows, :].astype(F32)
-        d = cot[rows, :].astype(F32) + gain_ref[0:1, frame] * e - h * inv[rows, 0:1]
+        d = cot[rows, :].astype(F32) + gain[0:1, frame] * e - h * inv[rows, 0:1]
         padded2[i + 1, 8:24, :] = d.astype(BF16).astype(F32)
         return total + e * h
 
@@ -351,6 +354,7 @@
     halo2 = send_edges(1)
     gather_act.forward()
     gather_pre = [gather_b(1, spread_pre[0]), gather_b(2, spread_pre[1])]
+    gather_cot.end()
 
     kall[0, y] = jnp.zeros((16, FR), F32)
     kall[0, y, 9:10, :] = jnp.sum(gain_sum, axis=0, keepdims=True)
@@ -368,6 +372,7 @@
             kall[0, y, k : k + 1, lanes] = jnp.sum(sums[k], axis=0, keepdims=True)
     k_copies = [send(kall.at[0, y], kall.at[0, y], at_y(d)) for d in (1, 2, 3)]
 
+    gather_pos.forward()
     arrived(halo2)
     fill_halo(padded2, 1)
     unshift = FR - shift
@@ -381,9 +386,6 @@
         return carry
 
     lax.fori_loop(0, ROWS, back_row, 0)
-    arrived(k_copies)
-    kall[1, z] = kall[0, 0] + kall[0, 1] + kall[0, 2] + kall[0, 3]
-    k_copies = [send(kall.at[1, z], kall.at[1, z], at_z(d)) for d in (1, 2, 3)]
 
     s = float(TOK * 32) ** -0.5
 
@@ -414,27 +416,28 @@
         own = local(ys[part].at[y], yr[part].at[y])
         return [send(ys[part].at[(y + d) % 4], yr[part].at[y], at_y(d)) for d in (1, 3, 2)], own
 
-    gather_cot.end()
     gather_act.end()
     gather_cot.ready()
     x_copy0 = product(0)
-    gather_pos.forward()
     for gather in gather_pre:
         gather.forward()
+    gather_pos.end()
     arrived(k_copies)
-    kall[2, xh] = kall[1, 0] + kall[1, 1] + kall[1, 2] + kall[1, 3]
-    k_copy = send(kall.at[2, xh], kall.at[2, xh], x_peer)
+    kall[1, z] = kall[0, 0] + kall[0, 1] + kall[0, 2] + kall[0, 3]
+    k_copies = [send(kall.at[1, z], kall.at[1, z], at_z(d)) for d in (1, 2, 3)]
     turns = [turn(0, x_copy0)]
-    gather_pos.end()
-    arrived([k_copy])
-    kg_ref[...] = pltpu.roll((kall[2, 0] + kall[2, 1]) * s, unshift, 1)
     gather_pos.ready()
     gather_pre[0].end()
     x_copy1 = product(1)
     gather_pre[1].end()
     x_copy2 = product(2)
+    arrived(k_copies)
+    kall[2, xh] = kall[1, 0] + kall[1, 1] + kall[1, 2] + kall[1, 3]
+    k_copy = send(kall.at[2, xh], kall.at[2, xh], x_peer)
     turns.append(turn(1, x_copy1))
     turns.append(turn(2, x_copy2))
+    arrived([k_copy])
+    kg_ref[...] = pltpu.roll((kall[2, 0] + kall[2, 1]) * s, unshift, 1)
     for copies, own in turns:
         arrived(copies)
         own.wait()
@@ -450,7 +453,7 @@
             out[:, k * HQ + first : k * HQ + first + count] = part[k, 0:100, :].astype(F32)
     for p in range(3):
         gk_ref[p] = small[3 * p : 3 * p + 3, 0:DQ]
-    gg_ref[...] = small[9:10, 0:DQ]
+    gg_ref[...] = small[9, 0:DQ]
 
 
 def on_device(tokens, cotangent, expand_weight, reduce_weight, position_kernel, norm_gain):
@@ -467,7 +470,7 @@
         in_specs=[vmem, vmem, hbm, hbm, vmem, vmem],
         out_specs=(vmem,) * 5,
         scratch_shapes=[
-            bf16(HD, D), bf16(HD, D),
+            bf16(HD, D), bf16(HD, D), f32(1, D),
             f32(10, 32, FR), f32(10, 32, FR),
             bf16(TOK, FR), bf16(TOK, FR),
             bf16(2, 4, FR, TOK),
@@ -491,7 +494,7 @@
             collective_id=0, has_side_effects=True, vmem_limit_bytes=60 * 2**20
         ),
         name="mlp_backward",
-    )(tokens, cotangent, expand_weight.T, reduce_weight.T, position_kernel, norm_gain.reshape(1, D))
+    )(tokens, cotangent, expand_weight.T, reduce_weight.T, position_kernel, norm_gain.reshape(25, 128))
     grad_tokens, grad_expand, grad_reduce, grad_kernel, grad_gain = pl.pallas_call(
         finish,
         out_shape=(
@@ -499,13 +502,13 @@
             jax.ShapeDtypeStruct((100, HD), F32),
             jax.ShapeDtypeStruct((100, HD), F32),
             jax.ShapeDtypeStruct((3, 3, DQ), F32),
-            jax.ShapeDtypeStruct((1, DQ), F32),
+            jax.ShapeDtypeStruct((DQ,), F32),
         ),
         in_specs=[vmem] * 5,
         out_specs=(vmem,) * 5,
         name="finish",
     )(gt, part0, part1, part2, small)
-    return grad_tokens, grad_expand, grad_reduce, grad_kernel, grad_gain.reshape(DQ)
+    return grad_tokens, grad_expand, grad_reduce, grad_kernel, grad_gain
 
 
 def solution(mesh):

time: 105 us -> 96.5 us (0.919)
  Pallas kernels: 102 us -> 95.5 us
  local copies, waits for them, and re-layouts: 1.33 us -> 0 us
  other arithmetic: 1.28 us -> 0 us
    pallas_call x1, Pallas kernels: 98.9 us -> 92.8 us  [on_device(): pl.pallas_call(kernel, out_shape=(jax.ShapeDtypeStruct((ROWS, COLS, DQ),...]
    reshape x1 -> x0, local copies, waits for them, and re-layouts: 1.33 us -> none  [on_device(): norm_gain.reshape(1, D)]
    pallas_call x1 -> x0, other arithmetic: 1.28 us -> none  [on_device(): pl.pallas_call(finish, out_shape=(jax.ShapeDtypeStruct((ROWS, COLS, DQ),...]
where the time goes in v3:
time: 96.5 us; the launch traced here: 96.1 us
  Pallas kernels  95.5 us (99%)
    pallas_call x1, Pallas kernels, on_device(): pl.pallas_call(kernel, out_shape=(jax.ShapeDtypeStruct((ROWS, COLS, DQ),...  92.8 us
    pallas_call x1, Pallas kernels, on_device(): pl.pallas_call(finish, out_shape=(jax.ShapeDtypeStruct((ROWS, COLS, DQ),...  2.63 us

profile of v3, /device:TPU:0, one launch (start us, length us, event | category | flops | bytes accessed | tf_op | source)
XLA Modules:
  0.0 96.1 jit_solution(16748561641234574525)
XLA Ops:
  0.6 92.8 %mlp_backward.1 = (bf16[8,16,800]{2,1,0:T(8,128)(2,1)}, bf16[4,112,400]{2,1,0:T(8,128)(2,1)}, bf16[4,112,256]{2,1,0:T(8,128)(2,1)}, bf16[4,112,144]{2,1,0:T(8,128)(2,1)}, f32[16,896]{1,0:T(8,128)}) custom-call(bf16[8,16,800]{2,1,0:T(8,128)(2,1)} %tok_ref.1, bf16[8,16,800]{2,1,0:T(8,128)(2,1)} %cot_ref.1, bf16[1600,3200]{1,0:T(8,128)(2,1)} %bitcast.3, ...), custom_call_target="tpu_custom_call" | custom-call | tf_op jit(solution)/shard_map/mlp_backward/pallas_call | solution.py:463
  93.5 2.6 %finish.1 = (bf16[8,16,800]{2,1,0:T(8,128)(2,1)}, f32[100,1600]{1,0:T(8,128)}, f32[100,1600]{1,0:T(8,128)}, f32[3,3,800]{2,1,0:T(4,128)}, f32[800]{0:T(1024)}) custom-call(bf16[8,16,800]{2,1,0:T(8,128)(2,1)} %get-tuple-element.10.gt_in, bf16[4,112,400]{2,1,0:T(8,128)(2,1)} %get-tuple-element.11.part0, bf16[4,112,256]{2,1,0:T(8,128)(2,1)} %get-tuple-element.12.part1, ...), custom_call_target="tpu_custom_call" | custom-call | tf_op jit(solution)/shard_map/finish/pallas_call | solution.py:498

commit v4 on v3

--- a/solution.py
+++ b/solution.py
@@ -313,79 +313,8 @@
 
     inner = lax.fori_loop(0, 25, gelu_tile, jnp.zeros((1, TOK), F32))
     spread_act = spread_b(0)
-    spread_pre = [spread_b(1), spread_b(2)]
     inn[1, tp] = jnp.broadcast_to(inner, (8, TOK))
     inner_copies = [send(inn.at[1, tp], inn.at[1, tp], to) for to in (sib, cross, far)]
-
-    for k in range(12):
-        b1[:, k * 128 : k * 128 + 128] = bt[1, k * 128 : k * 128 + 128, :].T
-    b1[:, 1536:1600] = bt[1, 1536:1600, :].T
-
-    def norm_chunk(j):
-        part = jnp.dot(b1[...], w1[:, pl.ds(mul(j * 768, 128), FR)], preferred_element_type=F32)
-        return part.astype(BF16)
-
-    e_copies = []
-    for k, (j, to) in enumerate(((tp_far, far), (tp_cross, cross), (tp_sib, sib))):
-        e_send[k] = norm_chunk(j)
-        e_copies.append(send(e_send.at[k], e_recv.at[tp], to))
-    e_recv[tp] = norm_chunk(tp)
-    gather_act = gather_b(0, spread_act)
-    gather_cot.forward()
-    gather_pos = gather_a(1, spread_pos)
-
-    arrived(inner_copies)
-    arrived(e_copies)
-    inner_row = inn[1, 0] + inn[1, 1] + inn[1, 2] + inn[1, 3]
-    factor = inner_row[0:1, :] * row_inv * row_inv * (1.0 / D)
-    inv[...] = jnp.broadcast_to(factor, (TOK, TOK)).T
-
-    def hidden_row(i, total):
-        rows = pl.ds(mul(i * COLS, 16), COLS)
-        e = e_recv[0, rows, :].astype(F32) + e_recv[1, rows, :].astype(F32)
-        e = e + e_recv[2, rows, :].astype(F32) + e_recv[3, rows, :].astype(F32)
-        h = pos[rows, :].astype(F32)
-        d = cot[rows, :].astype(F32) + gain[0:1, frame] * e - h * inv[rows, 0:1]
-        padded2[i + 1, 8:24, :] = d.astype(BF16).astype(F32)
-        return total + e * h
-
-    gain_sum = lax.fori_loop(0, ROWS, hidden_row, jnp.zeros((COLS, FR), F32))
-    fill_edges(padded2, 1)
-    halo2 = send_edges(1)
-    gather_act.forward()
-    gather_pre = [gather_b(1, spread_pre[0]), gather_b(2, spread_pre[1])]
-    gather_cot.end()
-
-    kall[0, y] = jnp.zeros((16, FR), F32)
-    kall[0, y, 9:10, :] = jnp.sum(gain_sum, axis=0, keepdims=True)
-    for n in range(7):
-        lanes = slice(n * 128, n * 128 + 128)
-
-        def taps(i, totals, lanes=lanes):
-            d = padded2[i + 1, 8:24, lanes]
-            return tuple(
-                totals[p * 3 + q] + d * padded[i + p, 7 + q : 23 + q, lanes] for p in range(3) for q in range(3)
-            )
-
-        sums = lax.fori_loop(0, ROWS, taps, tuple(jnp.zeros((COLS, 128), F32) for _ in range(9)))
-        for k in range(9):
-            kall[0, y, k : k + 1, lanes] = jnp.sum(sums[k], axis=0, keepdims=True)
-    k_copies = [send(kall.at[0, y], kall.at[0, y], at_y(d)) for d in (1, 2, 3)]
-
-    gather_pos.forward()
-    arrived(halo2)
-    fill_halo(padded2, 1)
-    unshift = FR - shift
-
-    def back_row(i, carry):
-        total = padded2[i + 1, 8:24, :]
-        for p in range(3):
-            for q in range(3):
-                total = total + pk_ref[p, q : q + 1, frame] * padded2[i + 2 - p, 9 - q : 25 - q, :]
-        gt_ref[i] = pltpu.roll(total, unshift, 1)[:, 0:DQ].astype(BF16)
-        return carry
-
-    lax.fori_loop(0, ROWS, back_row, 0)
 
     s = float(TOK * 32) ** -0.5
 
@@ -404,9 +333,10 @@
 
     def product(part):
         xs[part][...] = half(part, 1 - xh).astype(BF16)
-        copy = send(xs[part], xr[part], x_peer)
+        return send(xs[part], xr[part], x_peer)
+
+    def product_own(part):
         keep[part][...] = half(part, xh)
-        return copy
 
     def turn(part, copy):
         copy.wait_recv()
@@ -416,9 +346,82 @@
         own = local(ys[part].at[y], yr[part].at[y])
         return [send(ys[part].at[(y + d) % 4], yr[part].at[y], at_y(d)) for d in (1, 3, 2)], own
 
+
+    for k in range(12):
+        b1[:, k * 128 : k * 128 + 128] = bt[1, k * 128 : k * 128 + 128, :].T
+    b1[:, 1536:1600] = bt[1, 1536:1600, :].T
+
+    def norm_chunk(j):
+        part = jnp.dot(b1[...], w1[:, pl.ds(mul(j * 768, 128), FR)], preferred_element_type=F32)
+        return part.astype(BF16)
+
+    e_copies = []
+    for k, (j, to) in enumerate(((tp_far, far), (tp_cross, cross), (tp_sib, sib))):
+        e_send[k] = norm_chunk(j)
+        e_copies.append(send(e_send.at[k], e_recv.at[tp], to))
+    e_recv[tp] = norm_chunk(tp)
+    gather_act = gather_b(0, spread_act)
+    spread_pre = [spread_b(1), spread_b(2)]
+    gather_cot.forward()
+
+    arrived(inner_copies)
+    arrived(e_copies)
+    inner_row = inn[1, 0] + inn[1, 1] + inn[1, 2] + inn[1, 3]
+    factor = inner_row[0:1, :] * row_inv * row_inv * (1.0 / D)
+    inv[...] = jnp.broadcast_to(factor, (TOK, TOK)).T
+
+    def hidden_row(i, total):
+        rows = pl.ds(mul(i * COLS, 16), COLS)
+        e = e_recv[0, rows, :].astype(F32) + e_recv[1, rows, :].astype(F32)
+        e = e + e_recv[2, rows, :].astype(F32) + e_recv[3, rows, :].astype(F32)
+        h = pos[rows, :].astype(F32)
+        d = cot[rows, :].astype(F32) + gain[0:1, frame] * e - h * inv[rows, 0:1]
+        padded2[i + 1, 8:24, :] = d.astype(BF16).astype(F32)
+        return total + e * h
+
+    gather_pos = gather_a(1, spread_pos)
+    gain_sum = lax.fori_loop(0, ROWS, hidden_row, jnp.zeros((COLS, FR), F32))
+    fill_edges(padded2, 1)
+    halo2 = send_edges(1)
+    gather_act.forward()
+    gather_pre = [gather_b(1, spread_pre[0]), gather_b(2, spread_pre[1])]
+    gather_cot.end()
+
+    kall[0, y] = jnp.zeros((16, FR), F32)
+    kall[0, y, 9:10, :] = jnp.sum(gain_sum, axis=0, keepdims=True)
+    for n in range(7):
+        lanes = slice(n * 128, n * 128 + 128)
+
+        def taps(i, totals, lanes=lanes):
+            d = padded2[i + 1, 8:24, lanes]
+            return tuple(
+                totals[p * 3 + q] + d * padded[i + p, 7 + q : 23 + q, lanes] for p in range(3) for q in range(3)
+            )
+
+        sums = lax.fori_loop(0, ROWS, taps, tuple(jnp.zeros((COLS, 128), F32) for _ in range(9)))
+        for k in range(9):
+            kall[0, y, k : k + 1, lanes] = jnp.sum(sums[k], axis=0, keepdims=True)
+    k_copies = [send(kall.at[0, y], kall.at[0, y], at_y(d)) for d in (1, 2, 3)]
+
+    gather_pos.forward()
     gather_act.end()
     gather_cot.ready()
     x_copy0 = product(0)
+    product_own(0)
+    arrived(halo2)
+    fill_halo(padded2, 1)
+    unshift = FR - shift
+
+    def back_row(i, carry):
+        total = padded2[i + 1, 8:24, :]
+        for p in range(3):
+            for q in range(3):
+                total = total + pk_ref[p, q : q + 1, frame] * padded2[i + 2 - p, 9 - q : 25 - q, :]
+        gt_ref[i] = pltpu.roll(total, unshift, 1)[:, 0:DQ].astype(BF16)
+        return carry
+
+    lax.fori_loop(0, ROWS, back_row, 0)
+
     for gather in gather_pre:
         gather.forward()
     gather_pos.end()
@@ -431,6 +434,8 @@
     x_copy1 = product(1)
     gather_pre[1].end()
     x_copy2 = product(2)
+    product_own(1)
+    product_own(2)
     arrived(k_copies)
     kall[2, xh] = kall[1, 0] + kall[1, 1] + kall[1, 2] + kall[1, 3]
     k_copy = send(kall.at[2, xh], kall.at[2, xh], x_peer)

time: 96.5 us -> 95.1 us (0.985)
  Pallas kernels: 95.5 us -> 94.3 us
    pallas_call x1, Pallas kernels: 92.8 us -> 91.6 us  [on_device(): pl.pallas_call(kernel, out_shape=(jax.ShapeDtypeStruct((ROWS, COLS, DQ),...]
where the time goes in v4:
time: 95.1 us; the launch traced here: 94.9 us
  Pallas kernels  94.3 us (99%)
    pallas_call x1, Pallas kernels, on_device(): pl.pallas_call(kernel, out_shape=(jax.ShapeDtypeStruct((ROWS, COLS, DQ),...  91.6 us
    pallas_call x1, Pallas kernels, on_device(): pl.pallas_call(finish, out_shape=(jax.ShapeDtypeStruct((ROWS, COLS, DQ),...  2.63 us

profile of v4, /device:TPU:0, one launch (start us, length us, event | category | flops | bytes accessed | tf_op | source)
XLA Modules:
  0.0 94.9 jit_solution(17112509448890755459)
XLA Ops:
  0.6 91.6 %mlp_backward.1 = (bf16[8,16,800]{2,1,0:T(8,128)(2,1)}, bf16[4,112,400]{2,1,0:T(8,128)(2,1)}, bf16[4,112,256]{2,1,0:T(8,128)(2,1)}, bf16[4,112,144]{2,1,0:T(8,128)(2,1)}, f32[16,896]{1,0:T(8,128)}) custom-call(bf16[8,16,800]{2,1,0:T(8,128)(2,1)} %tok_ref.1, bf16[8,16,800]{2,1,0:T(8,128)(2,1)} %cot_ref.1, bf16[1600,3200]{1,0:T(8,128)(2,1)} %bitcast.3, ...), custom_call_target="tpu_custom_call" | custom-call | tf_op jit(solution)/shard_map/mlp_backward/pallas_call | solution.py:468
  92.3 2.6 %finish.1 = (bf16[8,16,800]{2,1,0:T(8,128)(2,1)}, f32[100,1600]{1,0:T(8,128)}, f32[100,1600]{1,0:T(8,128)}, f32[3,3,800]{2,1,0:T(4,128)}, f32[800]{0:T(1024)}) custom-call(bf16[8,16,800]{2,1,0:T(8,128)(2,1)} %get-tuple-element.10.gt_in, bf16[4,112,400]{2,1,0:T(8,128)(2,1)} %get-tuple-element.11.part0, bf16[4,112,256]{2,1,0:T(8,128)(2,1)} %get-tuple-element.12.part1, ...), custom_call_target="tpu_custom_call" | custom-call | tf_op jit(solution)/shard_map/finish/pallas_call | solution.py:503

commit v5 on v4

--- a/solution.py
+++ b/solution.py
@@ -239,10 +239,10 @@
             self.up.wait_recv()
             first = self.piece(below, 0)
             self.up = send(first, first, self.to(1))
+            self.to_sibling(self.block(below))
             self.down.wait_recv()
             second = self.piece(above, 1)
             self.down = send(second, second, self.to(3))
-            self.to_sibling(self.block(below))
             self.to_sibling(self.block(above))
 
         def end(self):

time: 95.1 us -> 95.1 us (level)
  no operation moved by 1% of the time
where the time goes in v5:
time: 95.1 us; the launch traced here: 94.9 us
  Pallas kernels  94.3 us (99%)
    pallas_call x1, Pallas kernels, on_device(): pl.pallas_call(kernel, out_shape=(jax.ShapeDtypeStruct((ROWS, COLS, DQ),...  91.6 us
    pallas_call x1, Pallas kernels, on_device(): pl.pallas_call(finish, out_shape=(jax.ShapeDtypeStruct((ROWS, COLS, DQ),...  2.63 us

profile of v5, /device:TPU:0, one launch (start us, length us, event | category | flops | bytes accessed | tf_op | source)
XLA Modules:
  0.0 94.9 jit_solution(7281769519991601628)
XLA Ops:
  0.6 91.6 %mlp_backward.1 = (bf16[8,16,800]{2,1,0:T(8,128)(2,1)}, bf16[4,112,400]{2,1,0:T(8,128)(2,1)}, bf16[4,112,256]{2,1,0:T(8,128)(2,1)}, bf16[4,112,144]{2,1,0:T(8,128)(2,1)}, f32[16,896]{1,0:T(8,128)}) custom-call(bf16[8,16,800]{2,1,0:T(8,128)(2,1)} %tok_ref.1, bf16[8,16,800]{2,1,0:T(8,128)(2,1)} %cot_ref.1, bf16[1600,3200]{1,0:T(8,128)(2,1)} %bitcast.3, ...), custom_call_target="tpu_custom_call" | custom-call | tf_op jit(solution)/shard_map/mlp_backward/pallas_call | solution.py:468
  92.3 2.6 %finish.1 = (bf16[8,16,800]{2,1,0:T(8,128)(2,1)}, f32[100,1600]{1,0:T(8,128)}, f32[100,1600]{1,0:T(8,128)}, f32[3,3,800]{2,1,0:T(4,128)}, f32[800]{0:T(1024)}) custom-call(bf16[8,16,800]{2,1,0:T(8,128)(2,1)} %get-tuple-element.10.gt_in, bf16[4,112,400]{2,1,0:T(8,128)(2,1)} %get-tuple-element.11.part0, bf16[4,112,256]{2,1,0:T(8,128)(2,1)} %get-tuple-element.12.part1, ...), custom_call_target="tpu_custom_call" | custom-call | tf_op jit(solution)/shard_map/finish/pallas_call | solution.py:503
